TPU v7x, 128 devices: a whole 4x4x4 slice. The times are simulated.
128 devices in a mesh: ctx: 16 (over y_lo, x, core), head: 8 (over z, y_hi).
Axes of the slice: x: 4, y: 4 (y_hi: 2, y_lo: 2; y = y_hi * 2 + y_lo), z: 4, core: 2. Of those that a mesh axis runs over, the one named last changes fastest.
Arguments:
- q_nope: bfloat16 [2048, 16384], P('ctx', 'head'), may hold values from -9 to 9
- q_rope: bfloat16 [2048, 8192], P('ctx', 'head'), may hold values from -200 to 200
- latent: bfloat16 [2048, 512], P('ctx'), may hold values from -350 to 350
- k_rope: bfloat16 [2048, 64], P('ctx'), may hold values from -3 to 3
- kv_gain: float32 [512], replicated, may hold values from 0.5 to 2
- w_uk: bfloat16 [512, 16384], P(None, 'head'), may hold values from -0.25 to 0.25
- w_uv: bfloat16 [512, 16384], P(None, 'head'), may hold values from -0.25 to 0.25
- w_out: bfloat16 [16384, 7168], P('head', 'ctx'), may hold values from -0.125 to 0.125
- block_pos: int32 [32], replicated, may hold values from 0 to 31, each once
Outputs:
- layer_out: bfloat16 [2048, 7168], P('head', 'ctx')
Inputs may be any that keep to these rules, and one draw needn't show every extreme that they name: Stored block j, rows j * 64 to (j + 1) * 64 - 1, holds the document's block block_pos[j]; every block number appears once.
All inputs are finite; a program needn't handle non-finite values.
Results may differ from a plain program's by a relative error of at most 0.018.
Values may be sent and summed in bfloat16 or wider, within the bound.
A program may use at most 128 MiB of HBM per device.

v0:
```python
import math

import jax
import jax.numpy as jnp
from jax import lax
from jax.sharding import PartitionSpec as P

NOPE = 128
ROPE = 64
VDIM = 128
BLK = 64


score_floor = -1e30


def passed_along(block, axis, distance):
    devices = range(lax.axis_size(axis))
    route = [((i - distance) % len(devices), i) for i in devices]
    return lax.ppermute(block, axis, route)


def row_positions(block_pos, first_row, row_count, block_rows):
    row_ids = first_row + jnp.arange(row_count, dtype=jnp.int32)
    block_ids = row_ids // block_rows
    block_table = jnp.arange(block_pos.shape[0], dtype=jnp.int32)
    matches = block_ids[:, None] == block_table[None, :]
    return (
        jnp.sum(jnp.where(matches, block_pos[None, :], 0), axis=1) * block_rows
        + row_ids % block_rows
    )


def normalize(latent, kv_gain):
    latent_f = latent.astype(jnp.float32)
    mean_square = jnp.mean(latent_f * latent_f, axis=1, keepdims=True)
    return (latent_f * lax.rsqrt(mean_square + 1e-06) * kv_gain[None, :]).astype(jnp.bfloat16)


def expand_flat(normed, w_uk, w_uv):
    key_flat = jnp.dot(normed, w_uk, preferred_element_type=jnp.float32).astype(jnp.bfloat16)
    value_flat = jnp.dot(normed, w_uv, preferred_element_type=jnp.float32).astype(jnp.bfloat16)
    return (key_flat, value_flat)


def shaped(key_flat, value_flat, rope_rows, key_pos, head_count):
    row_count = key_flat.shape[0]
    return (
        key_flat.reshape(row_count, head_count, NOPE),
        value_flat.reshape(row_count, head_count, VDIM),
        rope_rows,
        key_pos,
    )


def tile_update(carried, queries, key_set):
    run_max, row_total, accumulated = carried
    query_nope, query_rope, query_pos = queries
    key_nope, values, rope_rows, key_pos = key_set
    score_scale = 1.0 / math.sqrt(NOPE + ROPE)
    scores = jnp.einsum("thd,khd->thk", query_nope, key_nope, preferred_element_type=jnp.float32)
    scores = scores + jnp.einsum(
        "thd,kd->thk", query_rope, rope_rows, preferred_element_type=jnp.float32
    )
    scores = scores * score_scale
    admitted = (key_pos[None, :] <= query_pos[:, None])[:, None, :]
    scores = jnp.where(admitted, scores, score_floor)
    new_max = jnp.maximum(run_max, jnp.max(scores, axis=2))
    weights = jnp.where(admitted, jnp.exp(scores - new_max[:, :, None]), 0.0)
    factor = jnp.exp(run_max - new_max)
    row_total = row_total * factor + jnp.sum(weights, axis=2)
    accumulated = accumulated * factor[:, :, None] + jnp.einsum(
        "thk,khd->thd", weights.astype(jnp.bfloat16), values, preferred_element_type=jnp.float32
    )
    return (new_max, row_total, accumulated)


def attend(carried, queries, key_set):
    return tile_update(carried, queries, key_set)


def shards(q_nope, q_rope, latent, k_rope, kv_gain, w_uk, w_uv, w_out, block_pos):
    local_rows = q_nope.shape[0]
    head_count = w_uk.shape[1] // NOPE
    block_rows = BLK
    ctx_count = lax.axis_size("ctx")
    my_index = lax.axis_index("ctx")
    query_pos = row_positions(block_pos, my_index * local_rows, local_rows, block_rows)
    queries = (
        q_nope.reshape(local_rows, head_count, NOPE),
        q_rope.reshape(local_rows, head_count, ROPE),
        query_pos,
    )
    initial = (
        jnp.full((local_rows, head_count), score_floor, jnp.float32),
        jnp.zeros((local_rows, head_count), jnp.float32),
        jnp.zeros((local_rows, head_count, VDIM), jnp.float32),
    )
    normed = normalize(latent, kv_gain)

    def with_rows(carried, normed_rows, rope_rows, source):
        key_flat, value_flat = expand_flat(normed_rows, w_uk, w_uv)
        key_pos = row_positions(block_pos, source * local_rows, local_rows, block_rows)
        return attend(
            carried, queries, shaped(key_flat, value_flat, rope_rows, key_pos, head_count)
        )

    carried = with_rows(initial, normed, k_rope, my_index)

    def advance(turn_index, packed):
        held, normed_rows, rope_rows = packed
        normed_rows, rope_rows = passed_along((normed_rows, rope_rows), "ctx", 1)
        source = (my_index - turn_index - 1) % ctx_count
        return (with_rows(held, normed_rows, rope_rows, source), normed_rows, rope_rows)

    carried, normed, k_rope = lax.fori_loop(0, ctx_count - 1, advance, (carried, normed, k_rope))
    run_max, row_total, accumulated = carried
    attended = (
        (accumulated / row_total[:, :, None])
        .astype(jnp.bfloat16)
        .reshape(local_rows, head_count * VDIM)
    )
    partial_out = jnp.dot(
        lax.all_gather(attended, "ctx", axis=0, tiled=True),
        w_out,
        preferred_element_type=jnp.float32,
    )
    return lax.psum_scatter(
        partial_out.astype(jnp.bfloat16), "head", scatter_dimension=0, tiled=True
    )


def solution(mesh):
    placed = (
        P("ctx", "head"),
        P("ctx", "head"),
        P("ctx", None),
        P("ctx", None),
        P(),
        P(None, "head"),
        P(None, "head"),
        P("head", "ctx"),
        P(),
    )
    return jax.shard_map(
        shards, mesh=mesh, in_specs=placed, out_specs=P("head", "ctx"), check_vma=False
    )
```

profile of v0, /device:TPU:0, one launch (start us, length us, event | category | flops | bytes accessed | tf_op | source)
XLA Modules:
  0.0 411.9 jit_solution(9057265116941602596)
XLA Ops:
  16.3 2.9 fusion.19
  24.5 234.4 %while.24 = (s32[]{:T(128)}, f32[128,16]{0,1:T(8,128)}, f32[128,16]{0,1:T(8,128)}, f32[128,16,128]{0,2,1:T(8,128)}, bf16[128,512]{1,0:T(8,128)(2,1)S(1)}, /*inde...) while((s32[]{:T(128)}, f32[128,16]{0,1:T(8,128)}, ...), condition=%wide.region_8.9_spmd, body=%wide.region_4.8_spmd.sunk | while | flops 708349568 | bytes 25448664 | solution.py:116
  27.7 2.3 collective-permute-done.1
  33.8 2.1 fusion.77
  41.7 4.0 collective-permute-done.1
  57.3 4.0 collective-permute-done.1
  72.9 4.0 collective-permute-done.1
  88.5 4.0 collective-permute-done.1
  96.3 2.1 fusion.77
  104.2 4.0 collective-permute-done.1
  119.8 4.0 collective-permute-done.1
  135.4 4.0 collective-permute-done.1
  151.0 4.0 collective-permute-done.1
  166.7 4.0 collective-permute-done.1
  182.3 4.0 collective-permute-done.1
  190.0 2.1 fusion.77
  197.9 4.0 collective-permute-done.1
  213.5 4.0 collective-permute-done.1
  229.2 4.0 collective-permute-done.1
  244.8 4.0 collective-permute-done.1
  258.9 2.2 divide_convert_fusion
  261.2 60.5 %all-gather.2.cloned.1.call-done = bf16[2048,2048]{0,1:T(8,128)(2,1)} async-done(((bf16[128,2048]{0,1:T(8,128)(2,1)}), bf16[2048,2048]{0,1:T(8,128)(2,1)}) %all-gather.2.cloned.1.call-update) | async-done | bytes 8388624 | tf_op jit(solution)/shard_map/all_gather | solution.py:124
  321.7 8.4 %convolution_convert_fusion.2 = bf16[2048,448]{0,1:T(8,128)(2,1)} fusion(bf16[2048,448]{0,1:T(8,128)(2,1)S(1)} %copy-done, bf16[2048,2048]{0,1:T(8,128)(2,1)} %all-gather.2.cloned.1.call-done), kind=kOutput, calls=%fused_computation.31 | convolution fusion | flops 3759013888 | bytes 12058624 | tf_op jit(solution)/shard_map/dot_general | solution.py:123
  330.2 74.9 %reduce-scatter.2.cloned.1.call-done = bf16[256,448]{0,1:T(8,128)(2,1)} async-done(((bf16[2048,448]{0,1:T(8,128)(2,1)}), bf16[256,448]{0,1:T(8,128)(2,1)}) %reduce-scatter.2.cloned.1.call-update) | async-done | bytes 229392 | tf_op jit(solution)/shard_map/reduce_scatter | solution.py:128
  (521 shorter events, 182.8 us)
Async XLA Ops:
  6.5 315.2 %all-gather.2.cloned.1.call-start = ((), (), s32[]{:S(2)}) async-start(), calls=%async_computation.1 | async-start | bytes 8912896 | tf_op jit(solution)/shard_map/all_gather | solution.py:124
  24.5 6.9 %collective-permute-start = (bf16[128,512]{1,0:T(8,128)(2,1)S(1)}, bf16[128,512]{1,0:T(8,128)(2,1)S(1)}, u32[]{:S(2)}, u32[]{:S(2)}) collective-permute-start(bf16[128,512]{1,0:T(8,128)(2,1)S(1)} %get-tuple-element.533), channel_id=1, source_target_pairs={{120,0},{0,8},{8,16},{16,24},{24,32},{32,40},{40,48},{48,56},{56,6... | collective-permute-start | bytes 393224 | tf_op jit(solution)/shard_map/while/body/eval_jaxpr/ppermute | solution.py:20
  40.2 6.9 %collective-permute-start = (bf16[128,512]{1,0:T(8,128)(2,1)S(1)}, bf16[128,512]{1,0:T(8,128)(2,1)S(1)}, u32[]{:S(2)}, u32[]{:S(2)}) collective-permute-start(bf16[128,512]{1,0:T(8,128)(2,1)S(1)} %get-tuple-element.533), channel_id=1, source_target_pairs={{120,0},{0,8},{8,16},{16,24},{24,32},{32,40},{40,48},{48,56},{56,6... | collective-permute-start | bytes 393224 | tf_op jit(solution)/shard_map/while/body/eval_jaxpr/ppermute | solution.py:20
  55.8 6.9 %collective-permute-start = (bf16[128,512]{1,0:T(8,128)(2,1)S(1)}, bf16[128,512]{1,0:T(8,128)(2,1)S(1)}, u32[]{:S(2)}, u32[]{:S(2)}) collective-permute-start(bf16[128,512]{1,0:T(8,128)(2,1)S(1)} %get-tuple-element.533), channel_id=1, source_target_pairs={{120,0},{0,8},{8,16},{16,24},{24,32},{32,40},{40,48},{48,56},{56,6... | collective-permute-start | bytes 393224 | tf_op jit(solution)/shard_map/while/body/eval_jaxpr/ppermute | solution.py:20
  71.4 5.5 %collective-permute-start.1 = (bf16[128,64]{0,1:T(8,128)(2,1)}, bf16[128,64]{0,1:T(8,128)(2,1)S(1)}, u32[]{:S(2)}, u32[]{:S(2)}) collective-permute-start(bf16[128,64]{0,1:T(8,128)(2,1)} %get-tuple-element.534), channel_id=1, source_target_pairs={{120,0},{0,8},{8,16},{16,24},{24,32},{32,40},{40,48},{48,56},{56,6... | collective-permute-start | bytes 49160 | tf_op jit(solution)/shard_map/while/body/eval_jaxpr/ppermute | solution.py:20
  71.4 6.9 %collective-permute-start = (bf16[128,512]{1,0:T(8,128)(2,1)S(1)}, bf16[128,512]{1,0:T(8,128)(2,1)S(1)}, u32[]{:S(2)}, u32[]{:S(2)}) collective-permute-start(bf16[128,512]{1,0:T(8,128)(2,1)S(1)} %get-tuple-element.533), channel_id=1, source_target_pairs={{120,0},{0,8},{8,16},{16,24},{24,32},{32,40},{40,48},{48,56},{56,6... | collective-permute-start | bytes 393224 | tf_op jit(solution)/shard_map/while/body/eval_jaxpr/ppermute | solution.py:20
  87.0 5.5 %collective-permute-start.1 = (bf16[128,64]{0,1:T(8,128)(2,1)}, bf16[128,64]{0,1:T(8,128)(2,1)S(1)}, u32[]{:S(2)}, u32[]{:S(2)}) collective-permute-start(bf16[128,64]{0,1:T(8,128)(2,1)} %get-tuple-element.534), channel_id=1, source_target_pairs={{120,0},{0,8},{8,16},{16,24},{24,32},{32,40},{40,48},{48,56},{56,6... | collective-permute-start | bytes 49160 | tf_op jit(solution)/shard_map/while/body/eval_jaxpr/ppermute | solution.py:20
  87.0 6.9 %collective-permute-start = (bf16[128,512]{1,0:T(8,128)(2,1)S(1)}, bf16[128,512]{1,0:T(8,128)(2,1)S(1)}, u32[]{:S(2)}, u32[]{:S(2)}) collective-permute-start(bf16[128,512]{1,0:T(8,128)(2,1)S(1)} %get-tuple-element.533), channel_id=1, source_target_pairs={{120,0},{0,8},{8,16},{16,24},{24,32},{32,40},{40,48},{48,56},{56,6... | collective-permute-start | bytes 393224 | tf_op jit(solution)/shard_map/while/body/eval_jaxpr/ppermute | solution.py:20
  102.7 5.5 %collective-permute-start.1 = (bf16[128,64]{0,1:T(8,128)(2,1)}, bf16[128,64]{0,1:T(8,128)(2,1)S(1)}, u32[]{:S(2)}, u32[]{:S(2)}) collective-permute-start(bf16[128,64]{0,1:T(8,128)(2,1)} %get-tuple-element.534), channel_id=1, source_target_pairs={{120,0},{0,8},{8,16},{16,24},{24,32},{32,40},{40,48},{48,56},{56,6... | collective-permute-start | bytes 49160 | tf_op jit(solution)/shard_map/while/body/eval_jaxpr/ppermute | solution.py:20
  102.7 6.9 %collective-permute-start = (bf16[128,512]{1,0:T(8,128)(2,1)S(1)}, bf16[128,512]{1,0:T(8,128)(2,1)S(1)}, u32[]{:S(2)}, u32[]{:S(2)}) collective-permute-start(bf16[128,512]{1,0:T(8,128)(2,1)S(1)} %get-tuple-element.533), channel_id=1, source_target_pairs={{120,0},{0,8},{8,16},{16,24},{24,32},{32,40},{40,48},{48,56},{56,6... | collective-permute-start | bytes 393224 | tf_op jit(solution)/shard_map/while/body/eval_jaxpr/ppermute | solution.py:20
  118.3 5.5 %collective-permute-start.1 = (bf16[128,64]{0,1:T(8,128)(2,1)}, bf16[128,64]{0,1:T(8,128)(2,1)S(1)}, u32[]{:S(2)}, u32[]{:S(2)}) collective-permute-start(bf16[128,64]{0,1:T(8,128)(2,1)} %get-tuple-element.534), channel_id=1, source_target_pairs={{120,0},{0,8},{8,16},{16,24},{24,32},{32,40},{40,48},{48,56},{56,6... | collective-permute-start | bytes 49160 | tf_op jit(solution)/shard_map/while/body/eval_jaxpr/ppermute | solution.py:20
  118.3 6.9 %collective-permute-start = (bf16[128,512]{1,0:T(8,128)(2,1)S(1)}, bf16[128,512]{1,0:T(8,128)(2,1)S(1)}, u32[]{:S(2)}, u32[]{:S(2)}) collective-permute-start(bf16[128,512]{1,0:T(8,128)(2,1)S(1)} %get-tuple-element.533), channel_id=1, source_target_pairs={{120,0},{0,8},{8,16},{16,24},{24,32},{32,40},{40,48},{48,56},{56,6... | collective-permute-start | bytes 393224 | tf_op jit(solution)/shard_map/while/body/eval_jaxpr/ppermute | solution.py:20
  133.9 6.9 %collective-permute-start = (bf16[128,512]{1,0:T(8,128)(2,1)S(1)}, bf16[128,512]{1,0:T(8,128)(2,1)S(1)}, u32[]{:S(2)}, u32[]{:S(2)}) collective-permute-start(bf16[128,512]{1,0:T(8,128)(2,1)S(1)} %get-tuple-element.533), channel_id=1, source_target_pairs={{120,0},{0,8},{8,16},{16,24},{24,32},{32,40},{40,48},{48,56},{56,6... | collective-permute-start | bytes 393224 | tf_op jit(solution)/shard_map/while/body/eval_jaxpr/ppermute | solution.py:20
  149.5 6.9 %collective-permute-start = (bf16[128,512]{1,0:T(8,128)(2,1)S(1)}, bf16[128,512]{1,0:T(8,128)(2,1)S(1)}, u32[]{:S(2)}, u32[]{:S(2)}) collective-permute-start(bf16[128,512]{1,0:T(8,128)(2,1)S(1)} %get-tuple-element.533), channel_id=1, source_target_pairs={{120,0},{0,8},{8,16},{16,24},{24,32},{32,40},{40,48},{48,56},{56,6... | collective-permute-start | bytes 393224 | tf_op jit(solution)/shard_map/while/body/eval_jaxpr/ppermute | solution.py:20
  165.2 5.5 %collective-permute-start.1 = (bf16[128,64]{0,1:T(8,128)(2,1)}, bf16[128,64]{0,1:T(8,128)(2,1)S(1)}, u32[]{:S(2)}, u32[]{:S(2)}) collective-permute-start(bf16[128,64]{0,1:T(8,128)(2,1)} %get-tuple-element.534), channel_id=1, source_target_pairs={{120,0},{0,8},{8,16},{16,24},{24,32},{32,40},{40,48},{48,56},{56,6... | collective-permute-start | bytes 49160 | tf_op jit(solution)/shard_map/while/body/eval_jaxpr/ppermute | solution.py:20
  165.2 6.9 %collective-permute-start = (bf16[128,512]{1,0:T(8,128)(2,1)S(1)}, bf16[128,512]{1,0:T(8,128)(2,1)S(1)}, u32[]{:S(2)}, u32[]{:S(2)}) collective-permute-start(bf16[128,512]{1,0:T(8,128)(2,1)S(1)} %get-tuple-element.533), channel_id=1, source_target_pairs={{120,0},{0,8},{8,16},{16,24},{24,32},{32,40},{40,48},{48,56},{56,6... | collective-permute-start | bytes 393224 | tf_op jit(solution)/shard_map/while/body/eval_jaxpr/ppermute | solution.py:20
  180.8 5.5 %collective-permute-start.1 = (bf16[128,64]{0,1:T(8,128)(2,1)}, bf16[128,64]{0,1:T(8,128)(2,1)S(1)}, u32[]{:S(2)}, u32[]{:S(2)}) collective-permute-start(bf16[128,64]{0,1:T(8,128)(2,1)} %get-tuple-element.534), channel_id=1, source_target_pairs={{120,0},{0,8},{8,16},{16,24},{24,32},{32,40},{40,48},{48,56},{56,6... | collective-permute-start | bytes 49160 | tf_op jit(solution)/shard_map/while/body/eval_jaxpr/ppermute | solution.py:20
  180.8 6.9 %collective-permute-start = (bf16[128,512]{1,0:T(8,128)(2,1)S(1)}, bf16[128,512]{1,0:T(8,128)(2,1)S(1)}, u32[]{:S(2)}, u32[]{:S(2)}) collective-permute-start(bf16[128,512]{1,0:T(8,128)(2,1)S(1)} %get-tuple-element.533), channel_id=1, source_target_pairs={{120,0},{0,8},{8,16},{16,24},{24,32},{32,40},{40,48},{48,56},{56,6... | collective-permute-start | bytes 393224 | tf_op jit(solution)/shard_map/while/body/eval_jaxpr/ppermute | solution.py:20
  196.4 5.5 %collective-permute-start.1 = (bf16[128,64]{0,1:T(8,128)(2,1)}, bf16[128,64]{0,1:T(8,128)(2,1)S(1)}, u32[]{:S(2)}, u32[]{:S(2)}) collective-permute-start(bf16[128,64]{0,1:T(8,128)(2,1)} %get-tuple-element.534), channel_id=1, source_target_pairs={{120,0},{0,8},{8,16},{16,24},{24,32},{32,40},{40,48},{48,56},{56,6... | collective-permute-start | bytes 49160 | tf_op jit(solution)/shard_map/while/body/eval_jaxpr/ppermute | solution.py:20
  196.4 6.9 %collective-permute-start = (bf16[128,512]{1,0:T(8,128)(2,1)S(1)}, bf16[128,512]{1,0:T(8,128)(2,1)S(1)}, u32[]{:S(2)}, u32[]{:S(2)}) collective-permute-start(bf16[128,512]{1,0:T(8,128)(2,1)S(1)} %get-tuple-element.533), channel_id=1, source_target_pairs={{120,0},{0,8},{8,16},{16,24},{24,32},{32,40},{40,48},{48,56},{56,6... | collective-permute-start | bytes 393224 | tf_op jit(solution)/shard_map/while/body/eval_jaxpr/ppermute | solution.py:20
  212.0 6.9 %collective-permute-start = (bf16[128,512]{1,0:T(8,128)(2,1)S(1)}, bf16[128,512]{1,0:T(8,128)(2,1)S(1)}, u32[]{:S(2)}, u32[]{:S(2)}) collective-permute-start(bf16[128,512]{1,0:T(8,128)(2,1)S(1)} %get-tuple-element.533), channel_id=1, source_target_pairs={{120,0},{0,8},{8,16},{16,24},{24,32},{32,40},{40,48},{48,56},{56,6... | collective-permute-start | bytes 393224 | tf_op jit(solution)/shard_map/while/body/eval_jaxpr/ppermute | solution.py:20
  227.7 6.9 %collective-permute-start = (bf16[128,512]{1,0:T(8,128)(2,1)S(1)}, bf16[128,512]{1,0:T(8,128)(2,1)S(1)}, u32[]{:S(2)}, u32[]{:S(2)}) collective-permute-start(bf16[128,512]{1,0:T(8,128)(2,1)S(1)} %get-tuple-element.533), channel_id=1, source_target_pairs={{120,0},{0,8},{8,16},{16,24},{24,32},{32,40},{40,48},{48,56},{56,6... | collective-permute-start | bytes 393224 | tf_op jit(solution)/shard_map/while/body/eval_jaxpr/ppermute | solution.py:20
  243.3 6.9 %collective-permute-start = (bf16[128,512]{1,0:T(8,128)(2,1)S(1)}, bf16[128,512]{1,0:T(8,128)(2,1)S(1)}, u32[]{:S(2)}, u32[]{:S(2)}) collective-permute-start(bf16[128,512]{1,0:T(8,128)(2,1)S(1)} %get-tuple-element.533), channel_id=1, source_target_pairs={{120,0},{0,8},{8,16},{16,24},{24,32},{32,40},{40,48},{48,56},{56,6... | collective-permute-start | bytes 393224 | tf_op jit(solution)/shard_map/while/body/eval_jaxpr/ppermute | solution.py:20
  261.1 143.9 %reduce-scatter.2.cloned.1.call-start = ((), (), s32[]{:S(2)}) async-start(), calls=%async_computation.2 | async-start | bytes 2064384 | tf_op jit(solution)/shard_map/reduce_scatter | solution.py:128
  (116 other events, 545.3 us)
Sparse Core Ops, SparseCore 0:
  261.3 60.4 all-gather.1
  330.3 74.6 reduce-scatter.1
where the time goes:
time: 414 us; the launch traced here: 412 us
  waiting for transfers between devices  205 us (50%)
  matrix products  115 us (28%)
  local copies, waits for them, and re-layouts  41 us (10%)
  other arithmetic  32.4 us (8%)
  between operations  13.5 us (3%)
    reduce_scatter x1, waiting for transfers between devices, shards(): lax.psum_scatter(partial_out.astype(jnp.bfloat16), 'head', scatter_dimens...  74.9 us
    ppermute x30, waiting for transfers between devices, passed_along(): return lax.ppermute(block, axis, route)  70.1 us
    all_gather x1, waiting for transfers between devices, shards(): lax.all_gather(attended, 'ctx', axis=0, tiled=True)  60.5 us
    dot_general x16, matrix products, expand_flat(): jnp.dot(normed, w_uk, preferred_element_type=jnp.float32)  33.6 us
    while x255, local copies, waits for them, and re-layouts  32.9 us
    dot_general x16, matrix products, expand_flat(): jnp.dot(normed, w_uv, preferred_element_type=jnp.float32)  32.6 us
    dot_general x16, matrix products, tile_update(): jnp.einsum('thd,kd->thk', query_rope, rope_rows, preferred_element_type=j...  22.4 us
    reduce_sum x16, other arithmetic, row_positions(): jnp.sum(jnp.where(matches, block_pos[None, :], 0), axis=1) * block_rows  11.9 us
  transfers between devices with their start and end apart: 32, of which 32 were waited for; matrix products, arithmetic and copies ran while one was open for 8% of the time, Pallas kernels for 0%

commit v1 on v0

v1 whole, which is shorter than its diff:
```python
import functools
import math

import jax
import jax.numpy as jnp
from jax import lax
from jax.experimental import pallas as pl
from jax.experimental.pallas import tpu as pltpu
from jax.sharding import PartitionSpec as P

NOPE = 128
ROPE = 64
VDIM = 128
BLK = 64
FLOOR = -1e30
NT = (((1,), (1,)), ((), ()))
MESH = pl.DeviceIdType.MESH

YS, XS, CORES, ZS, YHS = 2, 4, 2, 4, 2
TO_Y, TO_XP, TO_XM, ON_XP, ON_XM, TO_CORE = 0, 1, 2, 3, 4, 5
GATHER_COPIES = TO_CORE + XS
TO_Z, TO_YH = 0, ZS - 1
SUM_COPIES = ZS


def dot32(a, b):
    return jnp.dot(a, b, preferred_element_type=jnp.float32)


def dot32_nt(a, b):
    return lax.dot_general(a, b, NT, preferred_element_type=jnp.float32)


def layer_kernel(
    heads,
    tokens,
    pos_ref,
    qn_ref,
    qr_ref,
    latent_ref,
    rope_ref,
    gain_ref,
    uk_ref,
    uv_ref,
    wo_ref,
    out_ref,
    kv,
    qa,
    att,
    part,
    zbuf,
    mine,
    ysend,
    ybuf,
    gsend,
    grecv,
    rsend,
    rrecv,
):
    rows = qn_ref.shape[0]
    rank = latent_ref.shape[1]
    width = kv.shape[-1]
    keys = YS * XS * CORES * rows
    chunks = rows // tokens
    exponent = math.log2(math.e) / math.sqrt(NOPE + ROPE)

    ctx = lax.axis_index("ctx")
    head_group = lax.axis_index("head")
    y, x, core = ctx // (XS * CORES), (ctx // CORES) % XS, ctx % CORES
    z, yh = head_group // YHS, head_group % YHS
    x_next, x_last, x_far = (x + 1) % XS, (x + XS - 1) % XS, (x + 2) % XS

    def at_ctx(y_, x_, core_):
        return ((y_ * XS + x_) * CORES + core_, head_group)

    def at_head(z_, yh_):
        return (ctx, z_ * YHS + yh_)

    across = at_ctx(1 - y, x, core)
    ahead = at_ctx(y, x_next, core)
    behind = at_ctx(y, x_last, core)
    sibling = at_ctx(y, x, 1 - core)
    over = at_head(z, 1 - yh)
    above = [at_head((z + k) % ZS, yh) for k in range(1, ZS)]

    barrier = pltpu.get_barrier_semaphore()
    partners = [across, ahead, behind, sibling, over] + above
    for partner in partners:
        pl.semaphore_signal(barrier, inc=1, device_id=partner, device_id_type=MESH)

    def remote(source, target, send, recv, partner):
        return pltpu.make_async_remote_copy(
            src_ref=source,
            dst_ref=target,
            send_sem=send,
            recv_sem=recv,
            device_id=partner,
            device_id_type=MESH,
        )

    def gather_copy(slots, turn, which):
        if which == TO_Y:
            view, partner = slots.at[y, x, core], across
        elif which == TO_XP:
            view, partner = slots.at[:, x, core], ahead
        elif which == TO_XM:
            view, partner = slots.at[:, x, core], behind
        elif which == ON_XP:
            view, partner = slots.at[0, x_last, core], ahead
        elif which == ON_XM:
            view, partner = slots.at[1, x_next, core], behind
        else:
            place = (x, x_last, x_next, x_far)[which - TO_CORE]
            view, partner = slots.at[:, place, core], sibling
        return remote(view, view, gsend.at[turn, which], grecv.at[turn, which], partner)

    def sum_copy(index, which):
        send, recv = rsend.at[index, which], rrecv.at[index, which]
        if which == TO_YH:
            return remote(ysend.at[index], ybuf.at[index], send, recv, over)
        return remote(
            part.at[index, (z + which + 1) % ZS], zbuf.at[index, which], send, recv, above[which]
        )

    def start(slots, turn, *copies):
        for which in copies:
            gather_copy(slots, turn, which).start()

    def arrived(slots, turn, *copies):
        for which in copies:
            gather_copy(slots, turn, which).wait_recv()

    latent = latent_ref[...].astype(jnp.float32)
    mean_square = jnp.mean(latent * latent, axis=1, keepdims=True)
    normed = (latent * lax.rsqrt(mean_square + 1e-06) * gain_ref[...]).astype(jnp.bfloat16)
    kv[y, x, core, :, :rank] = normed
    kv[y, x, core, :, rank:] = jnp.concatenate([rope_ref[...], rope_ref[...]], axis=1)

    pl.semaphore_wait(barrier, len(partners))
    start(kv, chunks, TO_Y)

    lane = lax.broadcasted_iota(jnp.int32, (rows, 2 * ROPE), 1)

    def project(head_list):
        for head in head_list:
            cols = slice(head * NOPE, (head + 1) * NOPE)
            mixed = dot32_nt(qn_ref[:, cols], uk_ref[:, cols]).astype(jnp.bfloat16)
            qa[:, head, :, :rank] = mixed.reshape(chunks, tokens, rank)
            pair = qr_ref[:, (head // 2) * 2 * ROPE : (head // 2 + 1) * 2 * ROPE]
            rope = jnp.where(lane // ROPE == head % 2, pair, jnp.zeros_like(pair))
            qa[:, head, :, rank:] = rope.reshape(chunks, tokens, 2 * ROPE)

    project(range(heads // 2))
    arrived(kv, chunks, TO_Y)
    start(kv, chunks, TO_XP, TO_XM, TO_CORE)
    project(range(heads // 2, heads))

    key_ids = lax.broadcasted_iota(jnp.int32, (tokens, keys), 1)
    key_pos = key_ids % BLK
    for block in range(keys // BLK):
        key_pos = jnp.where(key_ids // BLK == block, key_pos + pos_ref[block] * BLK, key_pos)

    arrived(kv, chunks, TO_XP, TO_XM)
    start(kv, chunks, ON_XP, ON_XM, TO_CORE + 1, TO_CORE + 2)
    arrived(kv, chunks, ON_XP, ON_XM)
    start(kv, chunks, TO_CORE + 3)
    arrived(kv, chunks, *range(TO_CORE, TO_CORE + XS))

    def attend(index):
        first = index * tokens
        first_pos = pos_ref[ctx * (rows // BLK) + first // BLK] * BLK + first % BLK
        query_pos = first_pos + lax.broadcasted_iota(jnp.int32, (tokens, keys), 0)
        bias = jnp.where(key_pos <= query_pos, 0.0, FLOOR)
        scores = dot32_nt(qa[index].reshape(heads * tokens, width), kv[...].reshape(keys, width))
        scores = scores.reshape(heads, tokens, keys) + bias[None]
        top = jnp.max(scores, axis=2, keepdims=True)
        weights = jnp.exp2((scores - top) * exponent)
        total = jnp.sum(weights, axis=2, keepdims=True)
        weights = weights.astype(jnp.bfloat16).reshape(heads * tokens, keys)
        mixed = dot32(weights, kv[:, :, :, :, :rank].reshape(keys, rank))
        mixed = (mixed.reshape(heads, tokens, rank) / total).astype(jnp.bfloat16)
        for head in range(heads):
            cols = slice(head * VDIM, (head + 1) * VDIM)
            att[index, y, x, core, :, cols] = dot32(mixed[head], uv_ref[:, cols]).astype(
                jnp.bfloat16
            )

    def step(turn, carry):
        def stage(delay, body):
            index = turn - delay

            @pl.when(jnp.logical_and(index >= 0, index < chunks))
            def _():
                body(index, att.at[index])

        def across_done(index, slots):
            arrived(slots, index, TO_Y)
            start(slots, index, TO_XP, TO_XM, TO_CORE)

        def along_done(index, slots):
            arrived(slots, index, TO_XP, TO_XM)
            start(slots, index, ON_XP, ON_XM, TO_CORE + 1, TO_CORE + 2)

        def onward_done(index, slots):
            arrived(slots, index, ON_XP, ON_XM)
            start(slots, index, TO_CORE + 3)

        def own(index, slots):
            attend(index)
            start(slots, index, TO_Y)

        def multiply(index, slots):
            arrived(slots, index, *range(TO_CORE, TO_CORE + XS))
            held = att[index].reshape(YS * XS * CORES * tokens, heads * VDIM)
            product = dot32(held, wo_ref[...]).astype(jnp.bfloat16)
            part[index] = product.reshape(ZS, YHS, CORES * tokens, product.shape[1])
            for which in range(ZS - 1):
                sum_copy(index, which).start()

        def sum_z(index, slots):
            for which in range(ZS - 1):
                sum_copy(index, which).wait_recv()

            def summed(half):
                value = part[index, z, half].astype(jnp.float32)
                for which in range(ZS - 1):
                    value += zbuf[index, which, half].astype(jnp.float32)
                return value

            ysend[index] = summed(1 - yh).astype(jnp.bfloat16)
            sum_copy(index, TO_YH).start()
            mine[index] = summed(yh)

        def finish(index, slots):
            sum_copy(index, TO_YH).wait_recv()
            value = (mine[index] + ybuf[index].astype(jnp.float32)).astype(jnp.bfloat16)
            for which in range(CORES):
                place = pl.ds(pl.multiple_of(which * rows + index * tokens, tokens), tokens)
                out_ref[place, :] = value[which * tokens : (which + 1) * tokens]

        stage(3, onward_done)
        stage(2, along_done)
        stage(1, across_done)
        stage(0, own)
        stage(4, multiply)
        stage(5, sum_z)
        stage(6, finish)
        return carry

    lax.fori_loop(0, chunks + 6, step, 0)

    for which in range(GATHER_COPIES):
        gather_copy(kv, chunks, which).wait_send()

    def drain(index, carry):
        for which in range(GATHER_COPIES):
            gather_copy(att.at[index], index, which).wait_send()
        for which in range(SUM_COPIES):
            sum_copy(index, which).wait_send()
        return carry

    lax.fori_loop(0, chunks, drain, 0)


TOKENS = 16


def shards(q_nope, q_rope, latent, k_rope, kv_gain, w_uk, w_uv, w_out, block_pos):
    rows = q_nope.shape[0]
    heads = w_uk.shape[1] // NOPE
    rank = latent.shape[1]
    width = rank + 2 * ROPE
    cols = w_out.shape[1]
    chunks = rows // TOKENS
    vmem = pl.BlockSpec(memory_space=pltpu.VMEM)
    smem = pl.BlockSpec(memory_space=pltpu.SMEM)
    return pl.pallas_call(
        functools.partial(layer_kernel, heads, TOKENS),
        name="layer",
        out_shape=jax.ShapeDtypeStruct((CORES * rows, cols), jnp.bfloat16),
        in_specs=[smem] + [vmem] * 8,
        out_specs=vmem,
        scratch_shapes=[
            pltpu.VMEM((YS, XS, CORES, rows, width), jnp.bfloat16),
            pltpu.VMEM((chunks, heads, TOKENS, width), jnp.bfloat16),
            pltpu.VMEM((chunks, YS, XS, CORES, TOKENS, heads * VDIM), jnp.bfloat16),
            pltpu.VMEM((chunks, ZS, YHS, CORES * TOKENS, cols), jnp.bfloat16),
            pltpu.VMEM((chunks, ZS - 1, YHS, CORES * TOKENS, cols), jnp.bfloat16),
            pltpu.VMEM((chunks, CORES * TOKENS, cols), jnp.float32),
            pltpu.VMEM((chunks, CORES * TOKENS, cols), jnp.bfloat16),
            pltpu.VMEM((chunks, CORES * TOKENS, cols), jnp.bfloat16),
            pltpu.SemaphoreType.DMA((chunks + 1, GATHER_COPIES)),
            pltpu.SemaphoreType.DMA((chunks + 1, GATHER_COPIES)),
            pltpu.SemaphoreType.DMA((chunks, SUM_COPIES)),
            pltpu.SemaphoreType.DMA((chunks, SUM_COPIES)),
        ],
        compiler_params=pltpu.CompilerParams(
            collective_id=0, has_side_effects=True, vmem_limit_bytes=60 * 2**20
        ),
    )(block_pos, q_nope, q_rope, latent, k_rope, kv_gain[None, :], w_uk, w_uv, w_out)


def solution(mesh):
    placed = (
        P("ctx", "head"),
        P("ctx", "head"),
        P("ctx", None),
        P("ctx", None),
        P(),
        P(None, "head"),
        P(None, "head"),
        P("head", "ctx"),
        P(),
    )
    return jax.shard_map(
        shards, mesh=mesh, in_specs=placed, out_specs=P("head", "ctx"), check_vma=False
    )
```

time: 414 us -> 109 us (0.26)
  waiting for transfers between devices: 205 us -> 0 us
  matrix products: 115 us -> 0 us
  Pallas kernels: 0 us -> 101 us
  local copies, waits for them, and re-layouts: 41 us -> 7.03 us
  other arithmetic: 32.4 us -> 0 us
  between operations: 13.5 us -> 0.01 us
    dot_general x81 -> x0, matrix products: 115 us -> none  [the longest x16 33.6 us: expand_flat(): jnp.dot(normed, w_uk, preferred_element_type=jnp.float32)]
    pallas_call x0 -> x1, Pallas kernels: none -> 101 us  [shards(): pl.pallas_call(functools.partial(layer_kernel, heads, TOKENS), name='laye...]
    reduce_scatter x1 -> x0, waiting for transfers between devices: 74.9 us -> none  [shards(): lax.psum_scatter(partial_out.astype(jnp.bfloat16), 'head', scatter_dimens...]
    ppermute x30 -> x0, waiting for transfers between devices: 70.1 us -> none  [passed_along(): return lax.ppermute(block, axis, route)]
    all_gather x1 -> x0, waiting for transfers between devices: 60.5 us -> none  [shards(): lax.all_gather(attended, 'ctx', axis=0, tiled=True)]
    while x256 -> x0, local copies, waits for them, and re-layouts: 33.1 us -> none
    reduce_sum x33 -> x0, other arithmetic: 16.1 us -> none  [the longest x16 11.9 us: row_positions(): jnp.sum(jnp.where(matches, block_pos[None, :], 0), axis=1) * block_rows]
    le x16 -> x0, other arithmetic: 11.4 us -> none  [tile_update(): admitted = (key_pos[None, :] <= query_pos[:, None])[:, None, :]]
  transfers between devices with their start and end apart: 32 -> 0, of which waited for: 32 -> 0; matrix products, arithmetic and copies ran while one was open for 8% -> 0% of each run, Pallas kernels for 0% -> 0%
where the time goes in v1:
time: 109 us; the launch traced here: 108 us
  Pallas kernels  101 us (93%)
  local copies, waits for them, and re-layouts  7.03 us (6%)
    pallas_call x1, Pallas kernels, shards(): pl.pallas_call(functools.partial(layer_kernel, heads, TOKENS), name='laye...  101 us
    unnamed x2, local copies, waits for them, and re-layouts  5.26 us

profile of v1, /device:TPU:0, one launch (start us, length us, event | category | flops | bytes accessed | tf_op | source)
XLA Modules:
  0.0 108.3 jit_solution(9042846506577763569)
XLA Ops:
  0.0 1.4 %copy.10.rope_ref = bf16[128,64]{1,0:T(8,128)(2,1)} copy(bf16[128,64]{0,1:T(8,128)(2,1)} %param.12) | data formatting | bytes 32768 | tf_op args[3]
  1.4 3.8 %copy.11.wo_ref = bf16[2048,448]{1,0:T(8,128)(2,1)} copy(bf16[2048,448]{0,1:T(8,128)(2,1)} %param.16) | data formatting | bytes 3670016 | tf_op args[7]
  5.3 101.2 %layer.1 = bf16[256,448]{1,0:T(8,128)(2,1)} custom-call(s32[32]{0:T(128)} %pos_ref.1, bf16[128,2048]{1,0:T(8,128)(2,1)} %qn_ref.1, bf16[128,1024]{1,0:T(8,128)(2,1)} %qr_ref.1, bf16[128,512]{1,0:T(8,128)(2,1)} %latent_ref.1, bf16[128,64]{1,0:T(8,128)(2,1)} %copy.10.rope_ref, f32[1,512]{1,0:T(1,128)} %bitcast.1, bf16[512,2048]{1,0:T(8,128)(2,1)} %uk_ref.1, ...), custom_call_target="tpu_custom_call" | custom-call | tf_op jit(solution)/shard_map/layer/pallas_call | solution.py:277
  106.5 1.8 %copy.12 = bf16[256,448]{0,1:T(8,128)(2,1)} copy(bf16[256,448]{1,0:T(8,128)(2,1)} %layer.1) | data formatting | bytes 458752 | tf_op jit(solution)/shard_map/layer/pallas_call | solution.py:277

commit v2 on v1

v2 whole, which is shorter than its diff:
```python
import functools
import math

import jax
import jax.numpy as jnp
from jax import lax
from jax.experimental import pallas as pl
from jax.experimental.pallas import tpu as pltpu
from jax.sharding import PartitionSpec as P

NOPE = 128
ROPE = 64
VDIM = 128
BLK = 64
FLOOR = -1e30
NT = (((1,), (1,)), ((), ()))
MESH = pl.DeviceIdType.MESH

YS, XS, CORES, ZS, YHS = 2, 4, 2, 4, 2
L_FAR, L_FAR_Y, L_XP, L_XM, L_Y1, L_Y2, L_YXP, L_YXM, L_Z, L_CORE = 0, 1, 2, 3, 4, 5, 6, 7, 8, 11
A_Y, A_XP, A_XM, A_ONP, A_ONM, A_CORE = range(6)
B_XP, B_XM, B_ONP, B_ONM, B_Y, B_CORE = 0, 1, 2, 3, 4, 8
LATENT_COPIES = L_CORE + XS
A_COPIES = A_CORE + XS
B_COPIES = B_CORE + YS
GATHER_COPIES = max(A_COPIES, B_COPIES)
B_EVERY, B_FIRST = 3, 2
TO_YH = ZS - 1
SUM_COPIES = ZS
LAST_COPIES = ZS * YHS - 1


def dot32(a, b):
    return jnp.dot(a, b, preferred_element_type=jnp.float32)


def dot32_nt(a, b):
    return lax.dot_general(a, b, NT, preferred_element_type=jnp.float32)


def layer_kernel(
    heads,
    tokens,
    pos_ref,
    qn_hbm,
    qr_hbm,
    latent_ref,
    rope_ref,
    gain_ref,
    uk_hbm,
    uv_hbm,
    wo_hbm,
    out_ref,
    qn_ref,
    qr_ref,
    uk_ref,
    uv_ref,
    wo_ref,
    kv,
    qa,
    att,
    part,
    zbuf,
    mine,
    ysend,
    ybuf,
    lastbuf,
    result,
    load_sem,
    lsend,
    lrecv,
    gsend,
    grecv,
    rsend,
    rrecv,
    fsend,
    frecv,
):
    loads = [
        pltpu.make_async_copy(source, target, load_sem.at[which])
        for which, (source, target) in enumerate(
            [
                (qn_hbm, qn_ref),
                (uk_hbm, uk_ref),
                (qr_hbm, qr_ref),
                (uv_hbm, uv_ref),
                (wo_hbm, wo_ref),
            ]
        )
    ]
    rows = qn_ref.shape[0]
    cols = out_ref.shape[0]
    rank = latent_ref.shape[1]
    width = kv.shape[-1]
    keys = YS * XS * CORES * rows
    chunks = rows // tokens
    exponent = math.log2(math.e) / math.sqrt(NOPE + ROPE)

    ctx = lax.axis_index("ctx")
    head_group = lax.axis_index("head")
    y, x, core = ctx // (XS * CORES), (ctx // CORES) % XS, ctx % CORES
    z, yh = head_group // YHS, head_group % YHS
    x_next, x_last, x_far = (x + 1) % XS, (x + XS - 1) % XS, (x + 2) % XS

    def at_ctx(y_, x_, core_):
        return ((y_ * XS + x_) * CORES + core_, head_group)

    def at_head(z_, yh_):
        return (ctx, z_ * YHS + yh_)

    across = at_ctx(1 - y, x, core)
    ahead = at_ctx(y, x_next, core)
    behind = at_ctx(y, x_last, core)
    sibling = at_ctx(y, x, 1 - core)
    far = at_ctx(y, x_far, core)
    far_across = at_ctx(1 - y, x_far, core)
    across_over = (across[0], at_head(z, 1 - yh)[1])
    others = [(k // YHS, k % YHS) for k in range(1, ZS * YHS)]
    groups = [at_head((z + dz) % ZS, (yh + dy) % YHS) for dz, dy in others]
    over = groups[0]
    above = [groups[YHS * k - 1] for k in range(1, ZS)]

    barrier = pltpu.get_barrier_semaphore()
    partners = [across, ahead, behind, sibling, far, far_across, across_over] + groups
    for partner in partners:
        pl.semaphore_signal(barrier, inc=1, device_id=partner, device_id_type=MESH)

    for load in loads:
        load.start()

    def remote(source, target, send, recv, partner):
        return pltpu.make_async_remote_copy(
            src_ref=source,
            dst_ref=target,
            send_sem=send,
            recv_sem=recv,
            device_id=partner,
            device_id_type=MESH,
        )

    def latent_copy(which):
        half = rows // 2
        own = kv.at[y, x, core]
        quarter = pl.ds(pl.multiple_of(z * (rows // ZS), rows // ZS), rows // ZS)
        if L_Z <= which < L_Z + ZS - 1:
            view, partner = kv.at[:, x_far, core, quarter], above[which - L_Z]
        else:
            view, partner = {
                L_FAR: (own.at[quarter], far),
                L_FAR_Y: (own.at[quarter], far_across),
                L_XP: (own, ahead),
                L_XM: (own, behind),
                L_Y1: (own.at[pl.ds(0, half)], across),
                L_Y2: (own.at[pl.ds(half, half)], across_over),
                L_YXP: (kv.at[1 - y, x, core], ahead),
                L_YXM: (kv.at[1 - y, x, core], behind),
                L_CORE: (kv.at[:, x, core], sibling),
                L_CORE + 1: (kv.at[:, x_last, core], sibling),
                L_CORE + 2: (kv.at[:, x_next, core], sibling),
                L_CORE + 3: (kv.at[:, x_far, core], sibling),
            }[which]
        return remote(view, view, lsend.at[which], lrecv.at[which], partner)

    def a_copy(index, which):
        slots = att.at[index]
        view, partner = {
            A_Y: (slots.at[y, x, core], across),
            A_XP: (slots.at[:, x, core], ahead),
            A_XM: (slots.at[:, x, core], behind),
            A_ONP: (slots.at[0, x_last, core], ahead),
            A_ONM: (slots.at[1, x_next, core], behind),
            A_CORE: (slots.at[:, x, core], sibling),
            A_CORE + 1: (slots.at[:, x_last, core], sibling),
            A_CORE + 2: (slots.at[:, x_next, core], sibling),
            A_CORE + 3: (slots.at[:, x_far, core], sibling),
        }[which]
        return remote(view, view, gsend.at[index, which], grecv.at[index, which], partner)

    def b_copy(index, which):
        slots = att.at[index]
        half = heads * VDIM // 2
        first, second = pl.ds(0, half), pl.ds(half, half)
        view, partner = {
            B_XP: (slots.at[y, x, core], ahead),
            B_XM: (slots.at[y, x, core], behind),
            B_ONP: (slots.at[y, x_last, core, :, first], ahead),
            B_ONM: (slots.at[y, x_next, core, :, second], behind),
            B_Y: (slots.at[y, x, core], across),
            B_Y + 1: (slots.at[y, x_last, core], across),
            B_Y + 2: (slots.at[y, x_next, core], across),
            B_Y + 3: (slots.at[y, x_far, core], across),
            B_CORE: (slots.at[y, :, core], sibling),
            B_CORE + 1: (slots.at[1 - y, :, core], sibling),
        }[which]
        return remote(view, view, gsend.at[index, which], grecv.at[index, which], partner)

    def sum_copy(index, which):
        send, recv = rsend.at[index, which], rrecv.at[index, which]
        if which == TO_YH:
            return remote(ysend.at[index], ybuf.at[index], send, recv, over)
        return remote(
            part.at[index, (z + which + 1) % ZS], zbuf.at[index, which], send, recv, above[which]
        )

    def last_copy(which):
        dz, dy = others[which]
        source = part.at[chunks - 1, (z + dz) % ZS, (yh + dy) % YHS]
        return remote(source, lastbuf.at[which], fsend.at[which], frecv.at[which], groups[which])

    def start(copy, *copies):
        for which in copies:
            copy(which).start()

    def arrived(copy, *copies):
        for which in copies:
            copy(which).wait_recv()

    latent = latent_ref[...].astype(jnp.float32)
    mean_square = jnp.mean(latent * latent, axis=1, keepdims=True)
    normed = (latent * lax.rsqrt(mean_square + 1e-06) * gain_ref[...]).astype(jnp.bfloat16)
    kv[y, x, core, :, :rank] = normed
    rope_key = rope_ref[...].astype(jnp.float32)
    rope_key = jnp.concatenate([rope_key, rope_key], axis=0).T
    kv[y, x, core, :, rank:] = rope_key.astype(jnp.bfloat16)

    lane = lax.broadcasted_iota(jnp.int32, (rows, 2 * ROPE), 1)

    def project(head_list):
        for head in head_list:
            span = slice(head * NOPE, (head + 1) * NOPE)
            mixed = dot32_nt(qn_ref[:, span], uk_ref[:, span]).astype(jnp.bfloat16)
            qa[:, head, :, :rank] = mixed.reshape(chunks, tokens, rank)
            pair = qr_ref[:, (head // 2) * 2 * ROPE : (head // 2 + 1) * 2 * ROPE]
            rope = jnp.where(lane // ROPE == head % 2, pair, jnp.zeros_like(pair))
            qa[:, head, :, rank:] = rope.reshape(chunks, tokens, 2 * ROPE)

    for load in loads[:3]:
        load.wait()
    project(range(heads // 2))
    pl.semaphore_wait(barrier, len(partners))
    start(latent_copy, L_FAR, L_FAR_Y, L_XP, L_XM, L_Y1, L_Y2)
    project(range(heads // 2, heads))

    key_ids = lax.broadcasted_iota(jnp.int32, (1, keys), 1)
    key_pos = key_ids % BLK
    for block in range(keys // BLK):
        key_pos = jnp.where(key_ids // BLK == block, key_pos + pos_ref[block] * BLK, key_pos)

    arrived(latent_copy, L_Y1, L_Y2)
    start(latent_copy, L_YXP, L_YXM)
    arrived(latent_copy, L_FAR, L_FAR_Y)
    start(latent_copy, L_Z, L_Z + 1, L_Z + 2, L_CORE)
    for load in loads[3:]:
        load.wait()
    arrived(latent_copy, L_XP, L_XM, L_YXP, L_YXM)
    start(latent_copy, L_CORE + 1, L_CORE + 2)
    arrived(latent_copy, L_Z, L_Z + 1, L_Z + 2)
    start(latent_copy, L_CORE + 3)
    arrived(latent_copy, *range(L_CORE, L_CORE + XS))

    def attend(index):
        first = index * tokens
        first_pos = pos_ref[ctx * (rows // BLK) + first // BLK] * BLK + first % BLK
        query_pos = first_pos + lax.broadcasted_iota(jnp.int32, (tokens, 1), 0)
        bias = jnp.where(key_pos <= query_pos, 0.0, FLOOR)
        scores = dot32_nt(qa[index].reshape(heads * tokens, width), kv[...].reshape(keys, width))
        scores = scores.reshape(heads, tokens, keys) + bias[None]
        top = jnp.max(scores, axis=2, keepdims=True)
        weights = jnp.exp2((scores - top) * exponent)
        total = jnp.sum(weights, axis=2, keepdims=True)
        weights = weights.astype(jnp.bfloat16).reshape(heads * tokens, keys)
        mixed = dot32(weights, kv[:, :, :, :, :rank].reshape(keys, rank))
        mixed = (mixed.reshape(heads, tokens, rank) / total).astype(jnp.bfloat16)
        for head in range(heads):
            span = slice(head * VDIM, (head + 1) * VDIM)
            att[index, y, x, core, :, span] = dot32(mixed[head], uv_ref[:, span]).astype(
                jnp.bfloat16
            )

    def a_own(index, copy):
        start(copy, A_Y)

    def a_across(index, copy):
        arrived(copy, A_Y)
        start(copy, A_XP, A_XM, A_CORE)

    def a_along(index, copy):
        arrived(copy, A_XP, A_XM)
        start(copy, A_ONP, A_ONM, A_CORE + 1, A_CORE + 2)

    def a_onward(index, copy):
        arrived(copy, A_ONP, A_ONM)
        start(copy, A_CORE + 3)

    def a_all(index, copy):
        arrived(copy, *range(A_CORE, A_CORE + XS))

    def b_own(index, copy):
        start(copy, B_XP, B_XM, B_Y)

    def b_along(index, copy):
        arrived(copy, B_XP, B_XM)
        start(copy, B_ONP, B_ONM, B_Y + 1, B_Y + 2)

    def b_onward(index, copy):
        arrived(copy, B_ONP, B_ONM)
        start(copy, B_Y + 3, B_CORE)

    def b_across(index, copy):
        arrived(copy, *range(B_Y, B_Y + XS))
        start(copy, B_CORE + 1)

    def b_all(index, copy):
        arrived(copy, *range(B_CORE, B_CORE + YS))

    def own(index, copy):
        attend(index)

    def multiply(index, copy):
        held = att[index].reshape(YS * XS * CORES * tokens, heads * VDIM)
        product = dot32_nt(held, wo_ref[...]).astype(jnp.bfloat16)
        part[index] = product.reshape(ZS, YHS, CORES * tokens, cols)
        if isinstance(index, int) and index == chunks - 1:
            start(last_copy, *range(LAST_COPIES))
        else:
            start(functools.partial(sum_copy, index), *range(ZS - 1))

    def sum_z(index, copy):
        for which in range(ZS - 1):
            sum_copy(index, which).wait_recv()

        def summed(half):
            value = part[index, z, half].astype(jnp.float32)
            for which in range(ZS - 1):
                value += zbuf[index, which, half].astype(jnp.float32)
            return value

        ysend[index] = summed(1 - yh).astype(jnp.bfloat16)
        sum_copy(index, TO_YH).start()
        mine[index] = summed(yh)

    def finish(index, copy):
        sum_copy(index, TO_YH).wait_recv()
        value = mine[index] + ybuf[index].astype(jnp.float32)
        place_rows(index, value)

    def place_rows(index, value):
        for which in range(CORES):
            place = pl.ds(pl.multiple_of(which * rows + index * tokens, tokens), tokens)
            result[place, :cols] = value[which * tokens : (which + 1) * tokens]

    def finish_last():
        arrived(last_copy, *range(LAST_COPIES))
        value = part[chunks - 1, z, yh].astype(jnp.float32)
        for which in range(LAST_COPIES):
            value += lastbuf[which].astype(jnp.float32)
        place_rows(chunks - 1, value)

    def sent(index):
        is_b = index % B_EVERY == B_FIRST
        copy = functools.partial(b_copy if is_b else a_copy, index)
        for which in range(B_COPIES if is_b else A_COPIES):
            copy(which).wait_send()
        for which in range(SUM_COPIES if index < chunks - 1 else 0):
            sum_copy(index, which).wait_send()

    def step(turn, carry):
        def stage(delay, body, kind=None):
            index = turn - delay
            due = index >= 0
            if kind is not None:
                due = jnp.logical_and(due, (index % B_EVERY == B_FIRST) == kind)

            @pl.when(due)
            def _():
                body(index, functools.partial(b_copy if kind else a_copy, index))

        stage(0, own)
        stage(0, a_own, False)
        stage(0, b_own, True)
        stage(1, a_across, False)
        stage(3, a_along, False)
        stage(3, b_along, True)
        stage(5, a_onward, False)
        stage(5, b_onward, True)
        stage(6, b_across, True)
        stage(6, a_all, False)
        stage(6, b_all, True)
        stage(6, multiply)
        stage(7, sum_z)
        return carry

    lax.fori_loop(0, chunks, step, 0)

    rest = [
        (b_along, 5),
        (a_onward, 3),
        (a_across, 7),
        (b_across, 2),
        (a_all, 3),
        (multiply, 3),
        (a_along, 6),
        (finish, 0),
        (a_onward, 4),
        (b_all, 2),
        (multiply, 2),
        (b_onward, 5),
        (sum_z, 1),
        (a_all, 4),
        (multiply, 4),
        (a_along, 7),
        (sum_z, 3),
        (b_across, 5),
        (a_onward, 6),
        (finish, 1),
        (sum_z, 2),
        (b_all, 5),
        (multiply, 5),
        (a_onward, 7),
        (finish, 3),
        (a_all, 6),
        (multiply, 6),
        (sum_z, 4),
        (a_all, 7),
        (multiply, 7),
        (finish, 2),
        (sum_z, 5),
        (finish, 4),
        (sum_z, 6),
        (finish, 5),
        (finish, 6),
    ]
    for body, index in rest:
        is_b = index % B_EVERY == B_FIRST
        body(index, functools.partial(b_copy if is_b else a_copy, index))
    for which in range(LATENT_COPIES):
        latent_copy(which).wait_send()
    for index in range(chunks):
        sent(index)
    finish_last()
    out_ref[...] = result[...].T[:cols].astype(jnp.bfloat16)
    for which in range(LAST_COPIES):
        last_copy(which).wait_send()


TOKENS = 16


def shards(q_nope, q_rope, latent, k_rope, kv_gain, w_uk, w_uv, w_out, block_pos):
    rows = q_nope.shape[0]
    heads = w_uk.shape[1] // NOPE
    rank = latent.shape[1]
    width = rank + 2 * ROPE
    cols = w_out.shape[1]
    chunks = rows // TOKENS
    vmem = pl.BlockSpec(memory_space=pltpu.VMEM)
    smem = pl.BlockSpec(memory_space=pltpu.SMEM)
    hbm = pl.BlockSpec(memory_space=pl.ANY)
    return pl.pallas_call(
        functools.partial(layer_kernel, heads, TOKENS),
        name="layer",
        out_shape=jax.ShapeDtypeStruct((cols, CORES * rows), jnp.bfloat16),
        in_specs=[smem, hbm, hbm, vmem, vmem, vmem, hbm, hbm, hbm],
        out_specs=vmem,
        scratch_shapes=[
            pltpu.VMEM(q_nope.shape, q_nope.dtype),
            pltpu.VMEM(q_rope.shape, q_rope.dtype),
            pltpu.VMEM(w_uk.shape, w_uk.dtype),
            pltpu.VMEM(w_uv.shape, w_uv.dtype),
            pltpu.VMEM((cols, heads * VDIM), w_out.dtype),
            pltpu.VMEM((YS, XS, CORES, rows, width), jnp.bfloat16),
            pltpu.VMEM((chunks, heads, TOKENS, width), jnp.bfloat16),
            pltpu.VMEM((chunks, YS, XS, CORES, TOKENS, heads * VDIM), jnp.bfloat16),
            pltpu.VMEM((chunks, ZS, YHS, CORES * TOKENS, cols), jnp.bfloat16),
            pltpu.VMEM((chunks, ZS - 1, YHS, CORES * TOKENS, cols), jnp.bfloat16),
            pltpu.VMEM((chunks, CORES * TOKENS, cols), jnp.float32),
            pltpu.VMEM((chunks, CORES * TOKENS, cols), jnp.bfloat16),
            pltpu.VMEM((chunks, CORES * TOKENS, cols), jnp.bfloat16),
            pltpu.VMEM((LAST_COPIES, CORES * TOKENS, cols), jnp.bfloat16),
            pltpu.VMEM((CORES * rows, pl.cdiv(cols, 128) * 128), jnp.float32),
            pltpu.SemaphoreType.DMA((5,)),
            pltpu.SemaphoreType.DMA((LATENT_COPIES,)),
            pltpu.SemaphoreType.DMA((LATENT_COPIES,)),
            pltpu.SemaphoreType.DMA((chunks, GATHER_COPIES)),
            pltpu.SemaphoreType.DMA((chunks, GATHER_COPIES)),
            pltpu.SemaphoreType.DMA((chunks, SUM_COPIES)),
            pltpu.SemaphoreType.DMA((chunks, SUM_COPIES)),
            pltpu.SemaphoreType.DMA((LAST_COPIES,)),
            pltpu.SemaphoreType.DMA((LAST_COPIES,)),
        ],
        compiler_params=pltpu.CompilerParams(
            collective_id=0, has_side_effects=True, vmem_limit_bytes=60 * 2**20
        ),
    )(block_pos, q_nope, q_rope, latent, k_rope.T, kv_gain[None, :], w_uk, w_uv, w_out.T).T


def solution(mesh):
    placed = (
        P("ctx", "head"),
        P("ctx", "head"),
        P("ctx", None),
        P("ctx", None),
        P(),
        P(None, "head"),
        P(None, "head"),
        P("head", "ctx"),
        P(),
    )
    return jax.shard_map(
        shards, mesh=mesh, in_specs=placed, out_specs=P("head", "ctx"), check_vma=False
    )
```

time: 109 us -> 79.8 us (0.73)
  Pallas kernels: 101 us -> 78 us
  local copies, waits for them, and re-layouts: 7.03 us -> 1.64 us
    pallas_call x1, Pallas kernels: 101 us -> 78 us  [shards(): pl.pallas_call(functools.partial(layer_kernel, heads, TOKENS), name='laye...]
    unnamed x2 -> x1, local copies, waits for them, and re-layouts: 5.26 us -> 1.64 us
    pallas_call x1 -> x0, local copies, waits for them, and re-layouts: 1.78 us -> none  [shards(): pl.pallas_call(functools.partial(layer_kernel, heads, TOKENS), name='laye...]
where the time goes in v2:
time: 79.8 us; the launch traced here: 79.7 us
  Pallas kernels  78 us (98%)
  local copies, waits for them, and re-layouts  1.64 us (2%)
    pallas_call x1, Pallas kernels, shards(): pl.pallas_call(functools.partial(layer_kernel, heads, TOKENS), name='laye...  78 us
    unnamed x1, local copies, waits for them, and re-layouts  1.64 us

profile of v2, /device:TPU:0, one launch (start us, length us, event | category | flops | bytes accessed | tf_op | source)
XLA Modules:
  0.0 79.7 jit_solution(17936278768750937127)
XLA Ops:
  0.0 78.0 %layer.1 = bf16[448,256]{1,0:T(8,128)(2,1)} custom-call(s32[32]{0:T(128)} %pos_ref.1, bf16[128,2048]{1,0:T(8,128)(2,1)} %qn_hbm.1, bf16[128,1024]{1,0:T(8,128)(2,1)} %qr_hbm.1, bf16[128,512]{1,0:T(8,128)(2,1)} %latent_ref.1, bf16[64,128]{1,0:T(8,128)(2,1)} %bitcast.6, f32[1,512]{1,0:T(1,128)} %bitcast.7, bf16[512,2048]{1,0:T(8,128)(2,1)} %uk_hbm.1, ...), custom_call_target="tpu_custom_call" | custom-call | tf_op jit(solution)/shard_map/layer/pallas_call | solution.py:459
  78.0 1.6 %copy.11 = bf16[256,448]{0,1:T(8,128)(2,1)} copy(bf16[256,448]{0,1:T(8,128)(2,1)} %bitcast.5) | data formatting | bytes 458752

commit v3 on v2

--- a/solution.py
+++ b/solution.py
@@ -20,11 +20,11 @@
 L_FAR, L_FAR_Y, L_XP, L_XM, L_Y1, L_Y2, L_YXP, L_YXM, L_Z, L_CORE = 0, 1, 2, 3, 4, 5, 6, 7, 8, 11
 A_Y, A_XP, A_XM, A_ONP, A_ONM, A_CORE = range(6)
 B_XP, B_XM, B_ONP, B_ONM, B_Y, B_CORE = 0, 1, 2, 3, 4, 8
-LATENT_COPIES = L_CORE + XS
+LATENT_COPIES = L_CORE + 6
 A_COPIES = A_CORE + XS
 B_COPIES = B_CORE + YS
 GATHER_COPIES = max(A_COPIES, B_COPIES)
-B_EVERY, B_FIRST = 3, 2
+X_FIRST = (1, 3, 5)
 TO_YH = ZS - 1
 SUM_COPIES = ZS
 LAST_COPIES = ZS * YHS - 1
@@ -41,16 +41,20 @@
 def layer_kernel(
     heads,
     tokens,
-    pos_ref,
+    pos_hbm,
     qn_hbm,
     qr_hbm,
-    latent_ref,
-    rope_ref,
-    gain_ref,
+    latent_hbm,
+    rope_hbm,
+    gain_hbm,
     uk_hbm,
     uv_hbm,
     wo_hbm,
     out_ref,
+    pos_ref,
+    latent_ref,
+    rope_ref,
+    gain_ref,
     qn_ref,
     qr_ref,
     uk_ref,
@@ -64,6 +68,7 @@
     mine,
     ysend,
     ybuf,
+    last_part,
     lastbuf,
     result,
     load_sem,
@@ -75,19 +80,8 @@
     rrecv,
     fsend,
     frecv,
+    greeted,
 ):
-    loads = [
-        pltpu.make_async_copy(source, target, load_sem.at[which])
-        for which, (source, target) in enumerate(
-            [
-                (qn_hbm, qn_ref),
-                (uk_hbm, uk_ref),
-                (qr_hbm, qr_ref),
-                (uv_hbm, uv_ref),
-                (wo_hbm, wo_ref),
-            ]
-        )
-    ]
     rows = qn_ref.shape[0]
     cols = out_ref.shape[0]
     rank = latent_ref.shape[1]
@@ -121,10 +115,26 @@
     above = [groups[YHS * k - 1] for k in range(1, ZS)]
 
     barrier = pltpu.get_barrier_semaphore()
-    partners = [across, ahead, behind, sibling, far, far_across, across_over] + groups
+    partners = [across, ahead, behind, sibling, far, far_across, across_over, above[0], above[2]]
     for partner in partners:
         pl.semaphore_signal(barrier, inc=1, device_id=partner, device_id_type=MESH)
 
+    loads = [
+        pltpu.make_async_copy(source, target, load_sem.at[which])
+        for which, (source, target) in enumerate(
+            [
+                (latent_hbm, latent_ref),
+                (gain_hbm, gain_ref),
+                (rope_hbm, rope_ref),
+                (qn_hbm, qn_ref),
+                (uk_hbm, uk_ref),
+                (qr_hbm, qr_ref),
+                (pos_hbm, pos_ref),
+                (uv_hbm, uv_ref),
+                (wo_hbm, wo_ref),
+            ]
+        )
+    ]
     for load in loads:
         load.start()
 
@@ -155,9 +165,11 @@
                 L_YXP: (kv.at[1 - y, x, core], ahead),
                 L_YXM: (kv.at[1 - y, x, core], behind),
                 L_CORE: (kv.at[:, x, core], sibling),
-                L_CORE + 1: (kv.at[:, x_last, core], sibling),
-                L_CORE + 2: (kv.at[:, x_next, core], sibling),
+                L_CORE + 1: (kv.at[y, x_last, core], sibling),
+                L_CORE + 2: (kv.at[y, x_next, core], sibling),
                 L_CORE + 3: (kv.at[:, x_far, core], sibling),
+                L_CORE + 4: (kv.at[1 - y, x_last, core], sibling),
+                L_CORE + 5: (kv.at[1 - y, x_next, core], sibling),
             }[which]
         return remote(view, view, lsend.at[which], lrecv.at[which], partner)
 
@@ -204,7 +216,7 @@
 
     def last_copy(which):
         dz, dy = others[which]
-        source = part.at[chunks - 1, (z + dz) % ZS, (yh + dy) % YHS]
+        source = last_part.at[(z + dz) % ZS, (yh + dy) % YHS]
         return remote(source, lastbuf.at[which], fsend.at[which], frecv.at[which], groups[which])
 
     def start(copy, *copies):
@@ -215,6 +227,8 @@
         for which in copies:
             copy(which).wait_recv()
 
+    for load in loads[:3]:
+        load.wait()
     latent = latent_ref[...].astype(jnp.float32)
     mean_square = jnp.mean(latent * latent, axis=1, keepdims=True)
     normed = (latent * lax.rsqrt(mean_square + 1e-06) * gain_ref[...]).astype(jnp.bfloat16)
@@ -234,11 +248,13 @@
             rope = jnp.where(lane // ROPE == head % 2, pair, jnp.zeros_like(pair))
             qa[:, head, :, rank:] = rope.reshape(chunks, tokens, 2 * ROPE)
 
-    for load in loads[:3]:
+    for load in loads[3:7]:
         load.wait()
     project(range(heads // 2))
     pl.semaphore_wait(barrier, len(partners))
     start(latent_copy, L_FAR, L_FAR_Y, L_XP, L_XM, L_Y1, L_Y2)
+    for neighbour in (above[0], above[2]):
+        pl.semaphore_signal(greeted, inc=1, device_id=neighbour, device_id_type=MESH)
     project(range(heads // 2, heads))
 
     key_ids = lax.broadcasted_iota(jnp.int32, (1, keys), 1)
@@ -249,14 +265,17 @@
     arrived(latent_copy, L_Y1, L_Y2)
     start(latent_copy, L_YXP, L_YXM)
     arrived(latent_copy, L_FAR, L_FAR_Y)
+    pl.semaphore_wait(greeted, 2)
     start(latent_copy, L_Z, L_Z + 1, L_Z + 2, L_CORE)
-    for load in loads[3:]:
+    for load in loads[7:]:
         load.wait()
-    arrived(latent_copy, L_XP, L_XM, L_YXP, L_YXM)
+    arrived(latent_copy, L_XP, L_XM)
     start(latent_copy, L_CORE + 1, L_CORE + 2)
+    arrived(latent_copy, L_YXP, L_YXM)
+    start(latent_copy, L_CORE + 4, L_CORE + 5)
     arrived(latent_copy, L_Z, L_Z + 1, L_Z + 2)
     start(latent_copy, L_CORE + 3)
-    arrived(latent_copy, *range(L_CORE, L_CORE + XS))
+    arrived(latent_copy, *range(L_CORE, LATENT_COPIES))
 
     def attend(index):
         first = index * tokens
@@ -313,31 +332,28 @@
     def b_all(index, copy):
         arrived(copy, *range(B_CORE, B_CORE + YS))
 
-    def own(index, copy):
-        attend(index)
-
     def multiply(index, copy):
         held = att[index].reshape(YS * XS * CORES * tokens, heads * VDIM)
         product = dot32_nt(held, wo_ref[...]).astype(jnp.bfloat16)
-        part[index] = product.reshape(ZS, YHS, CORES * tokens, cols)
+        product = product.reshape(ZS, YHS, CORES * tokens, cols)
         if isinstance(index, int) and index == chunks - 1:
+            last_part[...] = product
             start(last_copy, *range(LAST_COPIES))
         else:
+            part[index] = jnp.concatenate([product[:, 0], product[:, 1]], axis=2)
             start(functools.partial(sum_copy, index), *range(ZS - 1))
 
     def sum_z(index, copy):
         for which in range(ZS - 1):
             sum_copy(index, which).wait_recv()
 
-        def summed(half):
-            value = part[index, z, half].astype(jnp.float32)
-            for which in range(ZS - 1):
-                value += zbuf[index, which, half].astype(jnp.float32)
-            return value
-
-        ysend[index] = summed(1 - yh).astype(jnp.bfloat16)
+        value = part[index, z].astype(jnp.float32)
+        for which in range(ZS - 1):
+            value += zbuf[index, which].astype(jnp.float32)
+        lower, upper = value[:, :cols], value[:, cols:]
+        ysend[index] = jnp.where(yh == 0, upper, lower).astype(jnp.bfloat16)
         sum_copy(index, TO_YH).start()
-        mine[index] = summed(yh)
+        mine[index] = jnp.where(yh == 0, lower, upper)
 
     def finish(index, copy):
         sum_copy(index, TO_YH).wait_recv()
@@ -351,13 +367,13 @@
 
     def finish_last():
         arrived(last_copy, *range(LAST_COPIES))
-        value = part[chunks - 1, z, yh].astype(jnp.float32)
+        value = last_part[z, yh].astype(jnp.float32)
         for which in range(LAST_COPIES):
             value += lastbuf[which].astype(jnp.float32)
         place_rows(chunks - 1, value)
 
     def sent(index):
-        is_b = index % B_EVERY == B_FIRST
+        is_b = index in X_FIRST
         copy = functools.partial(b_copy if is_b else a_copy, index)
         for which in range(B_COPIES if is_b else A_COPIES):
             copy(which).wait_send()
@@ -365,74 +381,76 @@
             sum_copy(index, which).wait_send()
 
     def step(turn, carry):
-        def stage(delay, body, kind=None):
-            index = turn - delay
-            due = index >= 0
-            if kind is not None:
-                due = jnp.logical_and(due, (index % B_EVERY == B_FIRST) == kind)
-
-            @pl.when(due)
+        def stage(body, taken):
+            index = -1
+            for round_, chunk in enumerate(taken):
+                if chunk >= 0:
+                    index = jnp.where(turn == round_, chunk, index)
+
+            @pl.when(index >= 0)
             def _():
-                body(index, functools.partial(b_copy if kind else a_copy, index))
-
-        stage(0, own)
-        stage(0, a_own, False)
-        stage(0, b_own, True)
-        stage(1, a_across, False)
-        stage(3, a_along, False)
-        stage(3, b_along, True)
-        stage(5, a_onward, False)
-        stage(5, b_onward, True)
-        stage(6, b_across, True)
-        stage(6, a_all, False)
-        stage(6, b_all, True)
-        stage(6, multiply)
-        stage(7, sum_z)
+                copy = b_copy if body.__name__.startswith("b_") else a_copy
+                body(index, functools.partial(copy, index))
+
+        attend(turn)
+        stage(a_own, [-1 if k in X_FIRST else k for k in range(chunks)])
+        stage(b_own, [k if k in X_FIRST else -1 for k in range(chunks)])
+        stage(a_across, [-1, -1, 0, -1, 2, -1, 4, -1])
+        stage(b_onward, [-1, -1, -1, -1, -1, 1, -1, 3])
+        stage(a_along, [-1, -1, -1, -1, 0, -1, 2, -1])
+        stage(b_across, [-1, -1, -1, -1, -1, -1, -1, 1])
+        stage(b_along, [-1, -1, -1, 1, -1, 3, -1, 5])
+        stage(a_onward, [-1, -1, -1, -1, -1, -1, 0, -1])
         return carry
 
     lax.fori_loop(0, chunks, step, 0)
 
     rest = [
-        (b_along, 5),
-        (a_onward, 3),
+        (a_all, 0),
+        (multiply, 0),
+        (a_along, 4),
+        (b_all, 1),
+        (multiply, 1),
+        (a_across, 6),
+        (a_onward, 2),
+        (b_onward, 5),
         (a_across, 7),
-        (b_across, 2),
-        (a_all, 3),
-        (multiply, 3),
-        (a_along, 6),
-        (finish, 0),
+        (sum_z, 0),
         (a_onward, 4),
-        (b_all, 2),
+        (a_all, 2),
         (multiply, 2),
-        (b_onward, 5),
-        (sum_z, 1),
+        (b_across, 3),
         (a_all, 4),
         (multiply, 4),
+        (sum_z, 1),
+        (a_along, 6),
+        (b_all, 3),
+        (multiply, 3),
+        (b_across, 5),
+        (sum_z, 2),
+        (finish, 0),
         (a_along, 7),
-        (sum_z, 3),
-        (b_across, 5),
-        (a_onward, 6),
         (finish, 1),
-        (sum_z, 2),
         (b_all, 5),
         (multiply, 5),
+        (a_onward, 6),
+        (sum_z, 4),
+        (finish, 2),
         (a_onward, 7),
-        (finish, 3),
         (a_all, 6),
         (multiply, 6),
-        (sum_z, 4),
+        (sum_z, 3),
         (a_all, 7),
         (multiply, 7),
-        (finish, 2),
+        (finish, 4),
         (sum_z, 5),
-        (finish, 4),
+        (finish, 3),
         (sum_z, 6),
         (finish, 5),
         (finish, 6),
     ]
     for body, index in rest:
-        is_b = index % B_EVERY == B_FIRST
-        body(index, functools.partial(b_copy if is_b else a_copy, index))
+        body(index, functools.partial(b_copy if index in X_FIRST else a_copy, index))
     for which in range(LATENT_COPIES):
         latent_copy(which).wait_send()
     for index in range(chunks):
@@ -454,15 +472,18 @@
     cols = w_out.shape[1]
     chunks = rows // TOKENS
     vmem = pl.BlockSpec(memory_space=pltpu.VMEM)
-    smem = pl.BlockSpec(memory_space=pltpu.SMEM)
     hbm = pl.BlockSpec(memory_space=pl.ANY)
     return pl.pallas_call(
         functools.partial(layer_kernel, heads, TOKENS),
         name="layer",
         out_shape=jax.ShapeDtypeStruct((cols, CORES * rows), jnp.bfloat16),
-        in_specs=[smem, hbm, hbm, vmem, vmem, vmem, hbm, hbm, hbm],
+        in_specs=[hbm] * 9,
         out_specs=vmem,
         scratch_shapes=[
+            pltpu.SMEM(block_pos.shape, block_pos.dtype),
+            pltpu.VMEM(latent.shape, latent.dtype),
+            pltpu.VMEM(k_rope.shape[::-1], k_rope.dtype),
+            pltpu.VMEM((1, rank), kv_gain.dtype),
             pltpu.VMEM(q_nope.shape, q_nope.dtype),
             pltpu.VMEM(q_rope.shape, q_rope.dtype),
             pltpu.VMEM(w_uk.shape, w_uk.dtype),
@@ -471,14 +492,15 @@
             pltpu.VMEM((YS, XS, CORES, rows, width), jnp.bfloat16),
             pltpu.VMEM((chunks, heads, TOKENS, width), jnp.bfloat16),
             pltpu.VMEM((chunks, YS, XS, CORES, TOKENS, heads * VDIM), jnp.bfloat16),
-            pltpu.VMEM((chunks, ZS, YHS, CORES * TOKENS, cols), jnp.bfloat16),
-            pltpu.VMEM((chunks, ZS - 1, YHS, CORES * TOKENS, cols), jnp.bfloat16),
+            pltpu.VMEM((chunks, ZS, CORES * TOKENS, YHS * cols), jnp.bfloat16),
+            pltpu.VMEM((chunks, ZS - 1, CORES * TOKENS, YHS * cols), jnp.bfloat16),
             pltpu.VMEM((chunks, CORES * TOKENS, cols), jnp.float32),
             pltpu.VMEM((chunks, CORES * TOKENS, cols), jnp.bfloat16),
             pltpu.VMEM((chunks, CORES * TOKENS, cols), jnp.bfloat16),
+            pltpu.VMEM((ZS, YHS, CORES * TOKENS, cols), jnp.bfloat16),
             pltpu.VMEM((LAST_COPIES, CORES * TOKENS, cols), jnp.bfloat16),
             pltpu.VMEM((CORES * rows, pl.cdiv(cols, 128) * 128), jnp.float32),
-            pltpu.SemaphoreType.DMA((5,)),
+            pltpu.SemaphoreType.DMA((9,)),
             pltpu.SemaphoreType.DMA((LATENT_COPIES,)),
             pltpu.SemaphoreType.DMA((LATENT_COPIES,)),
             pltpu.SemaphoreType.DMA((chunks, GATHER_COPIES)),
@@ -487,6 +509,7 @@
             pltpu.SemaphoreType.DMA((chunks, SUM_COPIES)),
             pltpu.SemaphoreType.DMA((LAST_COPIES,)),
             pltpu.SemaphoreType.DMA((LAST_COPIES,)),
+            pltpu.SemaphoreType.REGULAR,
         ],
         compiler_params=pltpu.CompilerParams(
             collective_id=0, has_side_effects=True, vmem_limit_bytes=60 * 2**20

time: 79.8 us -> 73.6 us (0.922)
  Pallas kernels: 78 us -> 71.9 us
    pallas_call x1, Pallas kernels: 78 us -> 71.9 us  [shards(): pl.pallas_call(functools.partial(layer_kernel, heads, TOKENS), name='laye...]
where the time goes in v3:
time: 73.6 us; the launch traced here: 73.5 us
  Pallas kernels  71.9 us (98%)
  local copies, waits for them, and re-layouts  1.64 us (2%)
    pallas_call x1, Pallas kernels, shards(): pl.pallas_call(functools.partial(layer_kernel, heads, TOKENS), name='laye...  71.9 us
    unnamed x1, local copies, waits for them, and re-layouts  1.64 us

profile of v3, /device:TPU:0, one launch (start us, length us, event | category | flops | bytes accessed | tf_op | source)
XLA Modules:
  0.0 73.5 jit_solution(14230787045044502185)
XLA Ops:
  0.0 71.9 %layer.1 = bf16[448,256]{1,0:T(8,128)(2,1)} custom-call(s32[32]{0:T(128)} %pos_hbm.1, bf16[128,2048]{1,0:T(8,128)(2,1)} %qn_hbm.1, bf16[128,1024]{1,0:T(8,128)(2,1)} %qr_hbm.1, bf16[128,512]{1,0:T(8,128)(2,1)} %latent_hbm.1, bf16[64,128]{1,0:T(8,128)(2,1)} %bitcast.6, f32[1,512]{1,0:T(1,128)} %bitcast.7, bf16[512,2048]{1,0:T(8,128)(2,1)} %uk_hbm.1, ...), custom_call_target="tpu_custom_call" | custom-call | tf_op jit(solution)/shard_map/layer/pallas_call | solution.py:476
  71.9 1.6 %copy.11 = bf16[256,448]{0,1:T(8,128)(2,1)} copy(bf16[256,448]{0,1:T(8,128)(2,1)} %bitcast.5) | data formatting | bytes 458752

commit v4 on v3

--- a/solution.py
+++ b/solution.py
@@ -17,6 +17,8 @@
 MESH = pl.DeviceIdType.MESH
 
 YS, XS, CORES, ZS, YHS = 2, 4, 2, 4, 2
+SLOTS = ((0, 0), (1, 0), (0, 3), (0, 1), (1, 3), (1, 1), (0, 2), (1, 2))
+PACKED = 16
 L_FAR, L_FAR_Y, L_XP, L_XM, L_Y1, L_Y2, L_YXP, L_YXM, L_Z, L_CORE = 0, 1, 2, 3, 4, 5, 6, 7, 8, 11
 A_Y, A_XP, A_XM, A_ONP, A_ONM, A_CORE = range(6)
 B_XP, B_XM, B_ONP, B_ONM, B_Y, B_CORE = 0, 1, 2, 3, 4, 8
@@ -61,7 +63,10 @@
     uv_ref,
     wo_ref,
     kv,
+    rope_t,
+    pre,
     qa,
+    qr,
     att,
     part,
     zbuf,
@@ -85,7 +90,6 @@
     rows = qn_ref.shape[0]
     cols = out_ref.shape[0]
     rank = latent_ref.shape[1]
-    width = kv.shape[-1]
     keys = YS * XS * CORES * rows
     chunks = rows // tokens
     exponent = math.log2(math.e) / math.sqrt(NOPE + ROPE)
@@ -149,29 +153,29 @@
         )
 
     def latent_copy(which):
-        half = rows // 2
-        own = kv.at[y, x, core]
-        quarter = pl.ds(pl.multiple_of(z * (rows // ZS), rows // ZS), rows // ZS)
+        quarter = pl.ds(pl.multiple_of(z * (rank // ZS), rank // ZS), rank // ZS)
+        lower, upper = pl.ds(0, rank // 2), pl.ds(rank // 2, rank // 2)
         if L_Z <= which < L_Z + ZS - 1:
-            view, partner = kv.at[:, x_far, core, quarter], above[which - L_Z]
+            source = target = kv.at[pl.ds(6, 2), 0, :, quarter]
+            partner = above[which - L_Z]
         else:
-            view, partner = {
-                L_FAR: (own.at[quarter], far),
-                L_FAR_Y: (own.at[quarter], far_across),
-                L_XP: (own, ahead),
-                L_XM: (own, behind),
-                L_Y1: (own.at[pl.ds(0, half)], across),
-                L_Y2: (own.at[pl.ds(half, half)], across_over),
-                L_YXP: (kv.at[1 - y, x, core], ahead),
-                L_YXM: (kv.at[1 - y, x, core], behind),
-                L_CORE: (kv.at[:, x, core], sibling),
-                L_CORE + 1: (kv.at[y, x_last, core], sibling),
-                L_CORE + 2: (kv.at[y, x_next, core], sibling),
-                L_CORE + 3: (kv.at[:, x_far, core], sibling),
-                L_CORE + 4: (kv.at[1 - y, x_last, core], sibling),
-                L_CORE + 5: (kv.at[1 - y, x_next, core], sibling),
+            source, target, partner = {
+                L_FAR: (kv.at[0, 0, :, quarter], kv.at[6, 0, :, quarter], far),
+                L_FAR_Y: (kv.at[0, 0, :, quarter], kv.at[7, 0, :, quarter], far_across),
+                L_XP: (kv.at[0, 0], kv.at[2, 0], ahead),
+                L_XM: (kv.at[0, 0], kv.at[3, 0], behind),
+                L_Y1: (kv.at[0, 0, :, lower], kv.at[1, 0, :, lower], across),
+                L_Y2: (kv.at[0, 0, :, upper], kv.at[1, 0, :, upper], across_over),
+                L_YXP: (kv.at[1, 0], kv.at[4, 0], ahead),
+                L_YXM: (kv.at[1, 0], kv.at[5, 0], behind),
+                L_CORE: (kv.at[pl.ds(0, 2), 0], kv.at[pl.ds(0, 2), 1], sibling),
+                L_CORE + 1: (kv.at[2, 0], kv.at[2, 1], sibling),
+                L_CORE + 2: (kv.at[3, 0], kv.at[3, 1], sibling),
+                L_CORE + 3: (kv.at[pl.ds(6, 2), 0], kv.at[pl.ds(6, 2), 1], sibling),
+                L_CORE + 4: (kv.at[4, 0], kv.at[4, 1], sibling),
+                L_CORE + 5: (kv.at[5, 0], kv.at[5, 1], sibling),
             }[which]
-        return remote(view, view, lsend.at[which], lrecv.at[which], partner)
+        return remote(source, target, lsend.at[which], lrecv.at[which], partner)
 
     def a_copy(index, which):
         slots = att.at[index]
@@ -232,10 +236,9 @@
     latent = latent_ref[...].astype(jnp.float32)
     mean_square = jnp.mean(latent * latent, axis=1, keepdims=True)
     normed = (latent * lax.rsqrt(mean_square + 1e-06) * gain_ref[...]).astype(jnp.bfloat16)
-    kv[y, x, core, :, :rank] = normed
-    rope_key = rope_ref[...].astype(jnp.float32)
-    rope_key = jnp.concatenate([rope_key, rope_key], axis=0).T
-    kv[y, x, core, :, rank:] = rope_key.astype(jnp.bfloat16)
+    kv[0, 0, :rows] = normed
+    parts = [rope_ref[k * PACKED : (k + 1) * PACKED] for k in range(ROPE // PACKED)]
+    kv[0, 0, rows:] = jnp.concatenate(parts, axis=1)
 
     lane = lax.broadcasted_iota(jnp.int32, (rows, 2 * ROPE), 1)
 
@@ -243,10 +246,10 @@
         for head in head_list:
             span = slice(head * NOPE, (head + 1) * NOPE)
             mixed = dot32_nt(qn_ref[:, span], uk_ref[:, span]).astype(jnp.bfloat16)
-            qa[:, head, :, :rank] = mixed.reshape(chunks, tokens, rank)
+            qa[:, head] = mixed.reshape(chunks, tokens, rank)
             pair = qr_ref[:, (head // 2) * 2 * ROPE : (head // 2 + 1) * 2 * ROPE]
             rope = jnp.where(lane // ROPE == head % 2, pair, jnp.zeros_like(pair))
-            qa[:, head, :, rank:] = rope.reshape(chunks, tokens, 2 * ROPE)
+            qr[:, head] = rope.reshape(chunks, tokens, 2 * ROPE)
 
     for load in loads[3:7]:
         load.wait()
@@ -257,10 +260,47 @@
         pl.semaphore_signal(greeted, inc=1, device_id=neighbour, device_id_type=MESH)
     project(range(heads // 2, heads))
 
+    slots = YS * XS
+    early = slots // 2 * CORES * rows
     key_ids = lax.broadcasted_iota(jnp.int32, (1, keys), 1)
     key_pos = key_ids % BLK
-    for block in range(keys // BLK):
-        key_pos = jnp.where(key_ids // BLK == block, key_pos + pos_ref[block] * BLK, key_pos)
+    for slot, (dy, dx) in enumerate(SLOTS):
+        for side in range(CORES):
+            owner = ((y + dy) % YS * XS + (x + dx) % XS) * CORES + (core + side) % CORES
+            for k in range(rows // BLK):
+                here = key_ids // BLK == (slot * CORES + side) * (rows // BLK) + k
+                value = pos_ref[owner * (rows // BLK) + k] * BLK
+                key_pos = jnp.where(here, key_pos + value, key_pos)
+
+    def unpack_rope(slot_list):
+        for slot in slot_list:
+            for side in range(CORES):
+                held = kv[slot, side, rows:]
+                parts = [held[:, k * rows : (k + 1) * rows] for k in range(ROPE // PACKED)]
+                first = (slot * CORES + side) * rows
+                rope_t[:, first : first + rows] = jnp.concatenate(parts + parts, axis=0)
+
+    def score(queries, rope, first_slot, last_slot):
+        held = kv[first_slot:last_slot, :, :rows].reshape((last_slot - first_slot) * CORES * rows, rank)
+        span = slice(first_slot * CORES * rows, last_slot * CORES * rows)
+        return dot32_nt(queries, held) + dot32(rope, rope_t[:, span])
+
+    def score_early(first_slot, last_slot):
+        unpack_rope(range(first_slot, last_slot))
+        span = slice(first_slot * CORES * rows, last_slot * CORES * rows)
+
+        def pair(index, carry):
+            two = pl.ds(2 * index, 2)
+            value = score(
+                qa[two].reshape(2 * heads * tokens, rank),
+                qr[two].reshape(2 * heads * tokens, 2 * ROPE),
+                first_slot,
+                last_slot,
+            )
+            pre[two, :, span] = value.reshape(2, heads * tokens, value.shape[1])
+            return carry
+
+        lax.fori_loop(0, chunks // 2, pair, 0)
 
     arrived(latent_copy, L_Y1, L_Y2)
     start(latent_copy, L_YXP, L_YXM)
@@ -271,24 +311,33 @@
         load.wait()
     arrived(latent_copy, L_XP, L_XM)
     start(latent_copy, L_CORE + 1, L_CORE + 2)
+    arrived(latent_copy, L_CORE)
+    score_early(0, 2)
+    arrived(latent_copy, L_CORE + 1, L_CORE + 2)
+    score_early(2, 4)
     arrived(latent_copy, L_YXP, L_YXM)
     start(latent_copy, L_CORE + 4, L_CORE + 5)
     arrived(latent_copy, L_Z, L_Z + 1, L_Z + 2)
     start(latent_copy, L_CORE + 3)
-    arrived(latent_copy, *range(L_CORE, LATENT_COPIES))
+    arrived(latent_copy, L_CORE + 4, L_CORE + 5)
+    unpack_rope(range(4, 6))
+    arrived(latent_copy, L_CORE + 3)
+    unpack_rope(range(6, 8))
 
     def attend(index):
         first = index * tokens
         first_pos = pos_ref[ctx * (rows // BLK) + first // BLK] * BLK + first % BLK
         query_pos = first_pos + lax.broadcasted_iota(jnp.int32, (tokens, 1), 0)
         bias = jnp.where(key_pos <= query_pos, 0.0, FLOOR)
-        scores = dot32_nt(qa[index].reshape(heads * tokens, width), kv[...].reshape(keys, width))
+        queries = qa[index].reshape(heads * tokens, rank)
+        late = score(queries, qr[index].reshape(heads * tokens, 2 * ROPE), slots // 2, slots)
+        scores = jnp.concatenate([pre[index], late], axis=1)
         scores = scores.reshape(heads, tokens, keys) + bias[None]
         top = jnp.max(scores, axis=2, keepdims=True)
         weights = jnp.exp2((scores - top) * exponent)
         total = jnp.sum(weights, axis=2, keepdims=True)
         weights = weights.astype(jnp.bfloat16).reshape(heads * tokens, keys)
-        mixed = dot32(weights, kv[:, :, :, :, :rank].reshape(keys, rank))
+        mixed = dot32(weights, kv[:, :, :rows].reshape(keys, rank))
         mixed = (mixed.reshape(heads, tokens, rank) / total).astype(jnp.bfloat16)
         for head in range(heads):
             span = slice(head * VDIM, (head + 1) * VDIM)
@@ -372,13 +421,13 @@
             value += lastbuf[which].astype(jnp.float32)
         place_rows(chunks - 1, value)
 
-    def sent(index):
-        is_b = index in X_FIRST
-        copy = functools.partial(b_copy if is_b else a_copy, index)
-        for which in range(B_COPIES if is_b else A_COPIES):
-            copy(which).wait_send()
-        for which in range(SUM_COPIES if index < chunks - 1 else 0):
-            sum_copy(index, which).wait_send()
+    def gather_sent():
+        for which in range(LATENT_COPIES):
+            latent_copy(which).wait_send()
+        for index in range(chunks):
+            copy = functools.partial(b_copy if index in X_FIRST else a_copy, index)
+            for which in range(B_COPIES if index in X_FIRST else A_COPIES):
+                copy(which).wait_send()
 
     def step(turn, carry):
         def stage(body, taken):
@@ -395,12 +444,12 @@
         attend(turn)
         stage(a_own, [-1 if k in X_FIRST else k for k in range(chunks)])
         stage(b_own, [k if k in X_FIRST else -1 for k in range(chunks)])
+        stage(a_onward, [-1, -1, -1, -1, -1, -1, -1, 0])
+        stage(a_along, [-1, -1, -1, -1, -1, 0, -1, 2])
+        stage(b_across, [-1, -1, -1, -1, -1, -1, -1, 1])
         stage(a_across, [-1, -1, 0, -1, 2, -1, 4, -1])
         stage(b_onward, [-1, -1, -1, -1, -1, 1, -1, 3])
-        stage(a_along, [-1, -1, -1, -1, 0, -1, 2, -1])
-        stage(b_across, [-1, -1, -1, -1, -1, -1, -1, 1])
         stage(b_along, [-1, -1, -1, 1, -1, 3, -1, 5])
-        stage(a_onward, [-1, -1, -1, -1, -1, -1, 0, -1])
         return carry
 
     lax.fori_loop(0, chunks, step, 0)
@@ -415,11 +464,11 @@
         (a_onward, 2),
         (b_onward, 5),
         (a_across, 7),
-        (sum_z, 0),
-        (a_onward, 4),
         (a_all, 2),
         (multiply, 2),
+        (a_onward, 4),
         (b_across, 3),
+        (sum_z, 0),
         (a_all, 4),
         (multiply, 4),
         (sum_z, 1),
@@ -440,9 +489,9 @@
         (a_all, 6),
         (multiply, 6),
         (sum_z, 3),
+        (finish, 4),
         (a_all, 7),
         (multiply, 7),
-        (finish, 4),
         (sum_z, 5),
         (finish, 3),
         (sum_z, 6),
@@ -451,10 +500,11 @@
     ]
     for body, index in rest:
         body(index, functools.partial(b_copy if index in X_FIRST else a_copy, index))
-    for which in range(LATENT_COPIES):
-        latent_copy(which).wait_send()
-    for index in range(chunks):
-        sent(index)
+        if body is multiply and index == chunks - 1:
+            gather_sent()
+    for index in range(chunks - 1):
+        for which in range(SUM_COPIES):
+            sum_copy(index, which).wait_send()
     finish_last()
     out_ref[...] = result[...].T[:cols].astype(jnp.bfloat16)
     for which in range(LAST_COPIES):
@@ -468,7 +518,6 @@
     rows = q_nope.shape[0]
     heads = w_uk.shape[1] // NOPE
     rank = latent.shape[1]
-    width = rank + 2 * ROPE
     cols = w_out.shape[1]
     chunks = rows // TOKENS
     vmem = pl.BlockSpec(memory_space=pltpu.VMEM)
@@ -489,8 +538,11 @@
             pltpu.VMEM(w_uk.shape, w_uk.dtype),
             pltpu.VMEM(w_uv.shape, w_uv.dtype),
             pltpu.VMEM((cols, heads * VDIM), w_out.dtype),
-            pltpu.VMEM((YS, XS, CORES, rows, width), jnp.bfloat16),
-            pltpu.VMEM((chunks, heads, TOKENS, width), jnp.bfloat16),
+            pltpu.VMEM((YS * XS, CORES, rows + PACKED, rank), jnp.bfloat16),
+            pltpu.VMEM((2 * ROPE, YS * XS * CORES * rows), jnp.bfloat16),
+            pltpu.VMEM((chunks, heads * TOKENS, YS * XS * CORES * rows // 2), jnp.float32),
+            pltpu.VMEM((chunks, heads, TOKENS, rank), jnp.bfloat16),
+            pltpu.VMEM((chunks, heads, TOKENS, 2 * ROPE), jnp.bfloat16),
             pltpu.VMEM((chunks, YS, XS, CORES, TOKENS, heads * VDIM), jnp.bfloat16),
             pltpu.VMEM((chunks, ZS, CORES * TOKENS, YHS * cols), jnp.bfloat16),
             pltpu.VMEM((chunks, ZS - 1, CORES * TOKENS, YHS * cols), jnp.bfloat16),

time: 73.6 us -> 72.8 us (0.989)
  Pallas kernels: 71.9 us -> 71 us
    pallas_call x1, Pallas kernels: 71.9 us -> 71 us  [shards(): pl.pallas_call(functools.partial(layer_kernel, heads, TOKENS), name='laye...]
where the time goes in v4:
time: 72.8 us; the launch traced here: 72.7 us
  Pallas kernels  71 us (98%)
  local copies, waits for them, and re-layouts  1.64 us (2%)
    pallas_call x1, Pallas kernels, shards(): pl.pallas_call(functools.partial(layer_kernel, heads, TOKENS), name='laye...  71 us
    unnamed x1, local copies, waits for them, and re-layouts  1.64 us

profile of v4, /device:TPU:0, one launch (start us, length us, event | category | flops | bytes accessed | tf_op | source)
XLA Modules:
  0.0 72.7 jit_solution(3033875085226504258)
XLA Ops:
  0.0 71.0 %layer.1 = bf16[448,256]{1,0:T(8,128)(2,1)} custom-call(s32[32]{0:T(128)} %pos_hbm.1, bf16[128,2048]{1,0:T(8,128)(2,1)} %qn_hbm.1, bf16[128,1024]{1,0:T(8,128)(2,1)} %qr_hbm.1, bf16[128,512]{1,0:T(8,128)(2,1)} %latent_hbm.1, bf16[64,128]{1,0:T(8,128)(2,1)} %bitcast.6, f32[1,512]{1,0:T(1,128)} %bitcast.7, bf16[512,2048]{1,0:T(8,128)(2,1)} %uk_hbm.1, ...), custom_call_target="tpu_custom_call" | custom-call | tf_op jit(solution)/shard_map/layer/pallas_call | solution.py:525
  71.0 1.6 %copy.11 = bf16[256,448]{0,1:T(8,128)(2,1)} copy(bf16[256,448]{0,1:T(8,128)(2,1)} %bitcast.5) | data formatting | bytes 458752

commit v5 on v4

--- a/solution.py
+++ b/solution.py
@@ -390,7 +390,7 @@
             start(last_copy, *range(LAST_COPIES))
         else:
             part[index] = jnp.concatenate([product[:, 0], product[:, 1]], axis=2)
-            start(functools.partial(sum_copy, index), *range(ZS - 1))
+            start(functools.partial(sum_copy, index), 2, 1, 0)
 
     def sum_z(index, copy):
         for which in range(ZS - 1):
@@ -445,16 +445,16 @@
         stage(a_own, [-1 if k in X_FIRST else k for k in range(chunks)])
         stage(b_own, [k if k in X_FIRST else -1 for k in range(chunks)])
         stage(a_onward, [-1, -1, -1, -1, -1, -1, -1, 0])
-        stage(a_along, [-1, -1, -1, -1, -1, 0, -1, 2])
-        stage(b_across, [-1, -1, -1, -1, -1, -1, -1, 1])
+        stage(b_onward, [-1, -1, -1, -1, -1, 1, -1, 3])
         stage(a_across, [-1, -1, 0, -1, 2, -1, 4, -1])
-        stage(b_onward, [-1, -1, -1, -1, -1, 1, -1, 3])
         stage(b_along, [-1, -1, -1, 1, -1, 3, -1, 5])
+        stage(a_along, [-1, -1, -1, -1, 0, -1, 2, -1])
         return carry
 
     lax.fori_loop(0, chunks, step, 0)
 
     rest = [
+        (b_across, 1),
         (a_all, 0),
         (multiply, 0),
         (a_along, 4),

time: 72.8 us -> 72.6 us (level)
  no operation moved by 1% of the time
where the time goes in v5:
time: 72.6 us; the launch traced here: 72.5 us
  Pallas kernels  70.8 us (98%)
  local copies, waits for them, and re-layouts  1.64 us (2%)
    pallas_call x1, Pallas kernels, shards(): pl.pallas_call(functools.partial(layer_kernel, heads, TOKENS), name='laye...  70.8 us
    unnamed x1, local copies, waits for them, and re-layouts  1.64 us

profile of v5, /device:TPU:0, one launch (start us, length us, event | category | flops | bytes accessed | tf_op | source)
XLA Modules:
  0.0 72.5 jit_solution(4351154263447325793)
XLA Ops:
  0.0 70.8 %layer.1 = bf16[448,256]{1,0:T(8,128)(2,1)} custom-call(s32[32]{0:T(128)} %pos_hbm.1, bf16[128,2048]{1,0:T(8,128)(2,1)} %qn_hbm.1, bf16[128,1024]{1,0:T(8,128)(2,1)} %qr_hbm.1, bf16[128,512]{1,0:T(8,128)(2,1)} %latent_hbm.1, bf16[64,128]{1,0:T(8,128)(2,1)} %bitcast.6, f32[1,512]{1,0:T(1,128)} %bitcast.7, bf16[512,2048]{1,0:T(8,128)(2,1)} %uk_hbm.1, ...), custom_call_target="tpu_custom_call" | custom-call | tf_op jit(solution)/shard_map/layer/pallas_call | solution.py:525
  70.8 1.6 %copy.11 = bf16[256,448]{0,1:T(8,128)(2,1)} copy(bf16[256,448]{0,1:T(8,128)(2,1)} %bitcast.5) | data formatting | bytes 458752
